TPU v7x, 1024 devices: a whole 8x8x8 slice. The times are simulated.
1024 devices in a mesh: shard: 64 (over y, z), replica: 16 (over x, core).
Axes of the slice: x: 8, y: 8, z: 8, core: 2. Of those that a mesh axis runs over, the one named last changes fastest.
Arguments:
- grads: bfloat16 [16, 4096, 64, 256], P('replica', 'shard'), may hold values from -0.59765625 to 0.59765625
- slots: int32 [16, 64, 8, 4096], P('replica', 'shard'), may hold values from 0 to 1023
- lengths: int32 [16, 64, 4096], P('replica', 'shard'), may hold values from 1 to 8
- rows: float32 [65536, 256], P(('shard', 'replica')), may hold values from -6 to 6
- accum: float32 [65536], P(('shard', 'replica')), may hold values from 0.1 to 10
Outputs:
- new_rows: float32 [65536, 256], P(('shard', 'replica'))
- new_accum: float32 [65536], P(('shard', 'replica'))
- serving: bfloat16 [65536, 256], P('shard')
All inputs are finite; a program needn't handle non-finite values.
Results may differ from a plain program's by a relative error of at most 0.012.
Values may be sent and summed in bfloat16 or wider, within the bound.
No kernel may reach another device: no remote copies, remote signals or barrier semaphores. Data moves between devices by JAX's collectives and lax.ppermute only.
A program may use at most 32 MiB of HBM per device.

v0:
```python
import jax
import jax.numpy as jnp
from jax import lax
from jax.sharding import PartitionSpec as P

SLAB = 1024


step_rate = 0.5
epsilon = 1e-08


def rowwise_adagrad(row_grad, master, state):
    new_state = state + jnp.mean(row_grad * row_grad, axis=1)
    new_master = master - step_rate * row_grad / (jnp.sqrt(new_state)[:, None] + epsilon)
    return (new_master, new_state)


def shards(grads, slots, lengths, rows, accum):
    arrived = lax.all_to_all(grads, "shard", split_axis=2, concat_axis=1, tiled=True)
    total_samples = arrived.shape[1]
    feature_width = arrived.shape[3]
    pooled = arrived.reshape(total_samples, feature_width)
    slot_rows = slots.reshape(slots.shape[2], total_samples)
    bag_lens = lengths.reshape(total_samples)
    block_rows = min(512, total_samples)
    block_count = total_samples // block_rows

    def add_block(running, number):
        start = number * block_rows
        piece_grads = lax.dynamic_slice_in_dim(pooled, start, block_rows, 0)
        piece_slots = lax.dynamic_slice_in_dim(slot_rows, start, block_rows, 1)
        piece_lens = lax.dynamic_slice_in_dim(bag_lens, start, block_rows, 0)
        row_index = lax.broadcasted_iota(jnp.int32, (SLAB, block_rows), 0)
        counts = jnp.zeros((SLAB, block_rows), jnp.int32)
        for position in range(piece_slots.shape[0]):
            hits = (row_index == piece_slots[position][None, :]) & (position < piece_lens)[None, :]
            counts = counts + hits.astype(jnp.int32)
        product = jnp.dot(
            counts.astype(jnp.bfloat16), piece_grads, preferred_element_type=jnp.float32
        )
        return (running + product, None)

    initial = jnp.zeros((SLAB, feature_width), jnp.float32)
    partial_value, _ = lax.scan(add_block, initial, jnp.arange(block_count, dtype=jnp.int32))
    all_master, all_state = (
        lax.all_gather(rows, "replica", axis=0, tiled=True),
        lax.all_gather(accum, "replica", axis=0, tiled=True),
    )
    summed = lax.psum(partial_value.astype(jnp.bfloat16), "replica").astype(jnp.float32)
    new_master, new_state = rowwise_adagrad(summed, all_master, all_state)
    share = rows.shape[0]
    first = lax.axis_index("replica") * share
    new_rows = lax.dynamic_slice_in_dim(new_master, first, share, 0)
    new_accum = lax.dynamic_slice_in_dim(new_state, first, share, 0)
    serving = new_master.astype(jnp.bfloat16)
    return (new_rows, new_accum, serving)


def solution(mesh):
    return jax.shard_map(
        shards,
        mesh=mesh,
        in_specs=(
            P("replica", "shard", None, None),
            P("replica", "shard", None, None),
            P("replica", "shard", None),
            P(("shard", "replica"), None),
            P(("shard", "replica")),
        ),
        out_specs=(P(("shard", "replica"), None), P(("shard", "replica")), P("shard", None)),
        check_vma=False,
    )
```

profile of v0, /device:TPU:1, one launch (start us, length us, event | category | flops | bytes accessed | tf_op | source)
XLA Modules:
  0.0 316.1 jit_solution(922318555536069378)
XLA Ops:
  7.2 4.1 %copy.9 = bf16[1,64,64,256]{3,1,0,2:T(8,128)(2,1)} copy(bf16[1,64,64,256]{3,2,1,0:T(8,128)(2,1)} %param.7) | data formatting | bytes 4194304 | tf_op args[0]
  11.3 24.0 %all-to-all-start = ((bf16[1,64,64,256]{3,1,0,2:T(8,128)(2,1)}), bf16[1,64,64,256]{3,1,0,2:T(8,128)(2,1)S(1)}, u32[]{:S(2)}, u32[]{:S(2)}) async-start(bf16[1,64,64,256]{3,1,0,2:T(8,128)(2,1)} %copy.9), calls=%async_computation | async-start | bytes 4194304 | tf_op jit(solution)/shard_map/all_to_all | solution.py:20
  35.2 0.0 all-reduce.3.cloned.1.call-start
  35.3 48.4 %all-to-all-done = bf16[1,64,64,256]{3,1,0,2:T(8,128)(2,1)S(1)} async-done(((bf16[1,64,64,256]{3,1,0,2:T(8,128)(2,1)}), bf16[1,64,64,256]{3,1,0,2:T(8,128)(2,1)S(1)}, u32[]{:S(2)}, u32[]{:S(2)}) %all-to-all-start) | async-done | bytes 2097184 | tf_op jit(solution)/shard_map/all_to_all | solution.py:20
  83.7 49.0 %while.11 = (s32[]{:T(128)}, f32[1024,256]{1,0:T(8,128)S(1)}, s32[8]{0:T(128)S(1)}, s32[8,4096]{1,0:T(8,128)}, s32[4096]{0:T(1024)}, /*index=5*/bf16[4096,256]{1...) while((s32[]{:T(128)}, f32[1024,256]{1,0:T(8,128)S(1)}, ...), condition=%wide.region_1.2_spmd.clone, body=%wide.region_0.1_spmd.clone.sunk | while | flops 285741056 | bytes 2419037 | solution.py:45
  83.7 0.6 dynamic_slice.41
  85.0 1.1 constant_dynamic-slice_fusion.3
  86.1 0.8 broadcast_compare_fusion.9
  86.9 2.9 convolution_add_fusion.2
  89.8 0.6 dynamic_slice.41
  91.1 1.1 constant_dynamic-slice_fusion.3
  92.2 0.8 broadcast_compare_fusion.9
  93.0 2.9 convolution_add_fusion.2
  96.0 0.6 dynamic_slice.41
  97.2 1.1 constant_dynamic-slice_fusion.3
  98.3 0.8 broadcast_compare_fusion.9
  99.1 2.9 convolution_add_fusion.2
  102.1 0.6 dynamic_slice.41
  103.3 1.3 constant_dynamic-slice_fusion.3
  104.6 0.8 broadcast_compare_fusion.9
  105.4 2.9 convolution_add_fusion.2
  108.3 0.6 dynamic_slice.41
  109.6 1.1 constant_dynamic-slice_fusion.3
  110.7 0.8 broadcast_compare_fusion.9
  111.5 2.9 convolution_add_fusion.2
  114.4 0.6 dynamic_slice.41
  115.7 1.1 constant_dynamic-slice_fusion.3
  116.8 0.8 broadcast_compare_fusion.9
  117.6 2.9 convolution_add_fusion.2
  120.5 0.6 dynamic_slice.41
  121.8 1.1 constant_dynamic-slice_fusion.3
  122.9 0.8 broadcast_compare_fusion.9
  123.7 2.9 convolution_add_fusion.2
  126.6 0.6 dynamic_slice.41
  127.9 1.1 constant_dynamic-slice_fusion.3
  129.0 0.8 broadcast_compare_fusion.9
  129.8 2.9 convolution_add_fusion.2
  132.7 0.0 copy-start
  132.8 0.8 convert_element_type.36
  133.6 0.0 all-reduce.3.cloned.1.call-update
  133.6 0.0 all-gather.2.cloned.1.call-start
  133.7 0.7 all-gather.2.cloned.1.call-update
  134.4 1.3 dynamic-slice
  136.3 0.0 copy-done
  136.3 0.2 dynamic-update-slice
  136.6 27.3 %all-reduce = f32[1024]{0:T(1024)S(1)} all-reduce(f32[1024]{0:T(1024)S(1)} %dynamic-update-slice), channel_id=1, replica_groups=mesh['shard'=64,'replica'=16] {'replica'}, use_global_device_ids=true, to_apply=%add | all-reduce | flops 1024 | bytes 8192
  163.9 93.5 %all-reduce.3.cloned.1.call-done = bf16[1024,256]{1,0:T(8,128)(2,1)} async-done(((bf16[1024,256]{1,0:T(8,128)(2,1)}), bf16[1024,256]{1,0:T(8,128)(2,1)}) %all-reduce.3.cloned.1.call-update) | async-done | bytes 524304 | tf_op jit(solution)/shard_map/psum | solution.py:50
  257.3 1.3 fusion.28
  258.6 47.1 %all-gather.2.cloned.1.call-done = f32[1024,256]{1,0:T(8,128)} async-done(((f32[64,256]{1,0:T(8,128)}), f32[1024,256]{1,0:T(8,128)}) %all-gather.2.cloned.1.call-update) | async-done | bytes 1048592 | tf_op jit(solution)/shard_map/all_gather | solution.py:47
  305.7 2.4 fusion.29
  308.1 0.6 constant_dynamic-slice_fusion.1
  308.7 0.6 dynamic_slice.20
  (4 shorter events, 0.0 us)
Async XLA Ops:
  11.3 72.5 %all-to-all-start = ((bf16[1,64,64,256]{3,1,0,2:T(8,128)(2,1)}), bf16[1,64,64,256]{3,1,0,2:T(8,128)(2,1)S(1)}, u32[]{:S(2)}, u32[]{:S(2)}) async-start(bf16[1,64,64,256]{3,1,0,2:T(8,128)(2,1)} %copy.9), calls=%async_computation | async-start | bytes 4194304 | tf_op jit(solution)/shard_map/all_to_all | solution.py:20
  35.2 222.1 %all-reduce.3.cloned.1.call-start = ((), (), s32[]{:S(2)}) async-start(), calls=%async_computation.2 | async-start | bytes 1048576 | tf_op jit(solution)/shard_map/psum | solution.py:50
  132.7 3.6 %copy-start = (f32[64]{0:T(128)S(1)}, f32[64]{0:T(128)}, u32[]{:S(2)}) copy-start(f32[64]{0:T(128)} %param.11) | copy-start | bytes 772
  133.6 172.1 %all-gather.2.cloned.1.call-start = ((), (), s32[]{:S(2)}) async-start(), calls=%async_computation.1 | async-start | bytes 1114112 | tf_op jit(solution)/shard_map/all_gather | solution.py:47
Sparse Core Ops, SparseCore 0:
  133.8 123.5 all-reduce.2
  260.4 45.2 all-gather.1
where the time goes:
time: 317 us; the launch traced here: 316 us
  waiting for transfers between devices  190 us (60%)
  blocking collectives  27.3 us (9%)
  starting transfers between devices  24 us (8%)
  matrix products  23.5 us (7%)
  local copies, waits for them, and re-layouts  20.7 us (7%)
  between operations  14.8 us (5%)
  other arithmetic  10.7 us (3%)
  loops' own time  5.46 us (2%)
    psum x1, waiting for transfers between devices, shards(): lax.psum(partial_value.astype(jnp.bfloat16), 'replica').astype(jnp.float32)  93.5 us
    all_to_all x1, waiting for transfers between devices, shards(): lax.all_to_all(grads, 'shard', split_axis=2, concat_axis=1, tiled=True)  48.4 us
    all_gather x1, waiting for transfers between devices, shards(): lax.all_gather(rows, 'replica', axis=0, tiled=True)  47.1 us
    unnamed x1, blocking collectives  27.3 us
    all_to_all x1, starting transfers between devices, shards(): lax.all_to_all(grads, 'shard', split_axis=2, concat_axis=1, tiled=True)  24 us
    dot_general x8, matrix products, add_block(): jnp.dot(counts.astype(jnp.bfloat16), piece_grads, preferred_element_type=...  23.5 us
    slice x8, local copies, waits for them, and re-layouts, add_block(): piece_slots[position][None, :]  9.16 us
  transfers between devices with their start and end apart: 3, of which 3 were waited for; matrix products, arithmetic and copies ran while one was open for 1% of the time, Pallas kernels for 0%

commit v1 on v0

v1 whole, which is shorter than its diff:
```python
import jax
import jax.numpy as jnp
from jax import lax
from jax.experimental import pallas as pl
from jax.experimental.pallas import tpu as pltpu
from jax.sharding import PartitionSpec as P

SLAB = 1024
STEP_RATE = 0.5
EPSILON = 1e-08


def count_kernel(slots_ref, lens_ref, counts_ref):
    positions, width = slots_ref.shape
    slab = counts_ref.shape[0]
    tall = 64
    place = lax.broadcasted_iota(jnp.int32, (positions, width), 0)
    live = jnp.where(place < lens_ref[...], slots_ref[...], -1)
    ids = [
        jnp.broadcast_to(live[p : p + 1, :], (tall, width)).astype(jnp.int16)
        for p in range(positions)
    ]
    row = lax.broadcasted_iota(jnp.int32, (tall, width), 0).astype(jnp.int16)
    one = jnp.ones((tall, width), jnp.bfloat16)
    zero = jnp.zeros((tall, width), jnp.bfloat16)

    def rows_block(i, carry):
        first = i * tall
        mine = row + first.astype(jnp.int16)
        total = zero
        for p in range(positions):
            total = total + jnp.where(ids[p] == mine, one, zero)
        counts_ref[pl.ds(pl.multiple_of(first, tall), tall), :] = total
        return carry

    lax.fori_loop(0, slab // tall, rows_block, 0)


def count_matrix(slots, lens):
    positions, samples = slots.shape
    width = 256
    return pl.pallas_call(
        count_kernel,
        grid=(samples // width,),
        in_specs=[
            pl.BlockSpec((positions, width), lambda i: (0, i)),
            pl.BlockSpec((1, width), lambda i: (0, i)),
        ],
        out_specs=pl.BlockSpec((SLAB, width), lambda i: (0, i)),
        out_shape=jax.ShapeDtypeStruct((SLAB, samples), jnp.bfloat16),
        compiler_params=pltpu.CompilerParams(vmem_limit_bytes=16 * 1024 * 1024),
        cost_estimate=pl.CostEstimate(
            flops=16 * SLAB * samples, bytes_accessed=2 * SLAB * samples, transcendentals=0
        ),
        name="counts",
    )(slots, lens)


def shards(grads, slots, lengths, rows, accum):
    arrived = lax.all_to_all(grads, "shard", split_axis=2, concat_axis=1, tiled=True)
    samples, width = arrived.shape[1], arrived.shape[3]
    counts = count_matrix(slots.reshape(slots.shape[2], samples), lengths.reshape(1, samples))
    partial = jnp.dot(
        counts, arrived.reshape(samples, width), preferred_element_type=jnp.float32
    ).astype(jnp.bfloat16)
    share = rows.shape[0]
    parts = lax.all_to_all(
        partial.reshape(SLAB // share, share, width), "replica", 0, 0, tiled=True
    )
    row_grad = jnp.sum(parts.astype(jnp.float32), axis=0)
    new_accum = accum + jnp.mean(row_grad * row_grad, axis=1)
    new_rows = rows - STEP_RATE * row_grad / (jnp.sqrt(new_accum)[:, None] + EPSILON)
    serving = lax.all_gather(new_rows.astype(jnp.bfloat16), "replica", axis=0, tiled=True)
    return new_rows, new_accum, serving


def solution(mesh):
    return jax.shard_map(
        shards,
        mesh=mesh,
        in_specs=(
            P("replica", "shard", None, None),
            P("replica", "shard", None, None),
            P("replica", "shard", None),
            P(("shard", "replica"), None),
            P(("shard", "replica")),
        ),
        out_specs=(P(("shard", "replica"), None), P(("shard", "replica")), P("shard", None)),
        check_vma=False,
    )
```

time: 317 us -> 131 us (0.41)
  waiting for transfers between devices: 190 us -> 35.5 us
  matrix products: 23.5 us -> 5.74 us
  blocking collectives: 27.3 us -> 44.1 us
  between operations: 14.8 us -> 0.69 us
  local copies, waits for them, and re-layouts: 20.7 us -> 8.14 us
  Pallas kernels: 0 us -> 9.72 us
  other arithmetic: 10.7 us -> 1.41 us
  loops' own time: 5.46 us -> 0 us
    psum x1 -> x0, waiting for transfers between devices: 93.5 us -> none  [shards(): lax.psum(partial_value.astype(jnp.bfloat16), 'replica').astype(jnp.float32)]
    all_gather x1 -> x0, waiting for transfers between devices: 47.1 us -> none  [shards(): lax.all_gather(rows, 'replica', axis=0, tiled=True)]
    all_to_all x0 -> x1, blocking collectives: none -> 28.3 us  [shards(): lax.all_to_all(partial.reshape(SLAB // share, share, width), 'replica', 0...]
    unnamed x1 -> x0, blocking collectives: 27.3 us -> none
    dot_general x8 -> x1, matrix products: 23.5 us -> 5.74 us  [shards(): jnp.dot(counts, arrived.reshape(samples, width), preferred_element_type=j...]
    all_gather x0 -> x1, blocking collectives: none -> 15.9 us  [shards(): lax.all_gather(new_rows.astype(jnp.bfloat16), 'replica', axis=0, tiled=True)]
    all_to_all x1, waiting for transfers between devices: 48.4 us -> 35.5 us  [shards(): lax.all_to_all(grads, 'shard', split_axis=2, concat_axis=1, tiled=True)]
    pallas_call x0 -> x1, Pallas kernels: none -> 9.72 us  [count_matrix(): pl.pallas_call(count_kernel, grid=(samples // width,), in_specs=[pl.Block...]
  transfers between devices with their start and end apart: 3 -> 1, of which waited for: 3 -> 1; matrix products, arithmetic and copies ran while one was open for 1% -> 0% of each run, Pallas kernels for 0% -> 8%
where the time goes in v1:
time: 131 us; the launch traced here: 129 us
  blocking collectives  44.1 us (34%)
  waiting for transfers between devices  35.5 us (27%)
  starting transfers between devices  24.1 us (18%)
  Pallas kernels  9.72 us (7%)
  local copies, waits for them, and re-layouts  8.14 us (6%)
  matrix products  5.74 us (4%)
  other arithmetic  1.41 us (1%)
    all_to_all x1, waiting for transfers between devices, shards(): lax.all_to_all(grads, 'shard', split_axis=2, concat_axis=1, tiled=True)  35.5 us
    all_to_all x1, blocking collectives, shards(): lax.all_to_all(partial.reshape(SLAB // share, share, width), 'replica', 0...  28.3 us
    all_to_all x1, starting transfers between devices, shards(): lax.all_to_all(grads, 'shard', split_axis=2, concat_axis=1, tiled=True)  24.1 us
    all_gather x1, blocking collectives, shards(): lax.all_gather(new_rows.astype(jnp.bfloat16), 'replica', axis=0, tiled=True)  15.9 us
    pallas_call x1, Pallas kernels, count_matrix(): pl.pallas_call(count_kernel, grid=(samples // width,), in_specs=[pl.Block...  9.72 us
    unnamed x12, local copies, waits for them, and re-layouts  8.14 us
    dot_general x1, matrix products, shards(): jnp.dot(counts, arrived.reshape(samples, width), preferred_element_type=j...  5.74 us
  transfers between devices with their start and end apart: 1, of which 1 were waited for; matrix products, arithmetic and copies ran while one was open for 0% of the time, Pallas kernels for 8%

profile of v1, /device:TPU:1, one launch (start us, length us, event | category | flops | bytes accessed | tf_op | source)
XLA Modules:
  0.0 129.5 jit_solution(6660368034173933157)
XLA Ops:
  0.6 4.1 %copy.9 = bf16[1,64,64,256]{3,1,0,2:T(8,128)(2,1)} copy(bf16[1,64,64,256]{3,2,1,0:T(8,128)(2,1)} %param.5) | data formatting | bytes 4194304 | tf_op args[0]
  4.7 0.0 copy-start.1
  4.8 0.0 copy-start.2
  4.8 24.1 %all-to-all-start = ((bf16[1,64,64,256]{3,1,0,2:T(8,128)(2,1)}), bf16[1,64,64,256]{3,1,0,2:T(8,128)(2,1)S(1)}, u32[]{:S(2)}, u32[]{:S(2)}) async-start(bf16[1,64,64,256]{3,1,0,2:T(8,128)(2,1)} %copy.9), calls=%async_computation | async-start | bytes 4194304 | tf_op jit(solution)/shard_map/all_to_all | solution.py:60
  28.9 0.0 copy-done.1
  28.9 0.0 copy-done.2
  28.9 9.7 %counts.1 = bf16[1024,4096]{1,0:T(8,128)(2,1)S(1)} custom-call(s32[8,4096]{1,0:T(8,128)S(1)} %bitcast.10, s32[1,4096]{1,0:T(1,128)S(1)} %bitcast.11), custom_call_target="tpu_custom_call" | custom-call | flops 67108864 | bytes 8388608 | tf_op jit(solution)/shard_map/counts/pallas_call | solution.py:42
  38.6 0.0 copy-start
  38.6 3.2 %copy-done = bf16[1024,4096]{1,0:T(8,128)(2,1)} copy-done((bf16[1024,4096]{1,0:T(8,128)(2,1)}, bf16[1024,4096]{1,0:T(8,128)(2,1)S(1)}, u32[]{:S(2)}) %copy-start) | copy-done | bytes 8388632
  41.8 35.5 %all-to-all-done = bf16[1,64,64,256]{3,1,0,2:T(8,128)(2,1)S(1)} async-done(((bf16[1,64,64,256]{3,1,0,2:T(8,128)(2,1)}), bf16[1,64,64,256]{3,1,0,2:T(8,128)(2,1)S(1)}, u32[]{:S(2)}, u32[]{:S(2)}) %all-to-all-start) | async-done | bytes 2097184 | tf_op jit(solution)/shard_map/all_to_all | solution.py:60
  77.4 0.0 copy-start.4
  77.4 0.0 copy-start.3
  77.4 5.7 %convolution_convert_fusion = bf16[1024,256]{1,0:T(8,128)(2,1)S(1)} fusion(bf16[1024,4096]{1,0:T(8,128)(2,1)} %copy-done, bf16[4096,256]{1,0:T(8,128)(2,1)S(1)} %bitcast.12), kind=kOutput, calls=%fused_computation | convolution fusion | flops 2147745792 | bytes 11010048 | tf_op jit(solution)/shard_map/dot_general | solution.py:63
  83.1 28.3 %all_to_all.20 = bf16[16,64,256]{2,1,0:T(8,128)(2,1)S(1)} all-to-all(bf16[16,64,256]{2,1,0:T(8,128)(2,1)S(1)} %bitcast.13), channel_id=1, replica_groups=mesh['shard'=64,'replica'=16] {'replica'}, dimensions={0} | all-to-all | bytes 1048576 | tf_op jit(solution)/shard_map/all_to_all | solution.py:67
  111.4 0.1 convert_reduce_fusion
  111.4 0.1 multiply_reduce_fusion
  111.5 0.0 copy-done.4
  111.6 0.5 sqrt_add_fusion
  112.1 0.0 copy-done.3
  112.1 0.7 fusion
  112.8 15.9 %all_gather.3 = bf16[1024,256]{1,0:T(8,128)(2,1)S(1)} all-gather(bf16[64,256]{1,0:T(8,128)(2,1)S(1)} %get-tuple-element.3), channel_id=1, replica_groups=mesh['shard'=64,'replica'=16] {'replica'}, dimensions={0}, use_global_device_ids=true | all-gather | bytes 557056 | tf_op jit(solution)/shard_map/all_gather | solution.py:73
  128.7 0.8 copy.11
Async XLA Ops:
  4.7 24.1 %copy-start.1 = (s32[1,1,8,4096]{3,2,1,0:T(8,128)S(1)}, s32[1,1,8,4096]{3,2,1,0:T(8,128)}, u32[]{:S(2)}) copy-start(s32[1,1,8,4096]{3,2,1,0:T(8,128)} %param.6) | copy-start | bytes 393220
  4.8 24.1 %copy-start.2 = (s32[1,1,4096]{2,1,0:T(1,128)S(1)}, s32[1,1,4096]{2,1,0:T(1,128)}, u32[]{:S(2)}) copy-start(s32[1,1,4096]{2,1,0:T(1,128)} %param.7) | copy-start | bytes 49156
  4.8 72.6 %all-to-all-start = ((bf16[1,64,64,256]{3,1,0,2:T(8,128)(2,1)}), bf16[1,64,64,256]{3,1,0,2:T(8,128)(2,1)S(1)}, u32[]{:S(2)}, u32[]{:S(2)}) async-start(bf16[1,64,64,256]{3,1,0,2:T(8,128)(2,1)} %copy.9), calls=%async_computation | async-start | bytes 4194304 | tf_op jit(solution)/shard_map/all_to_all | solution.py:60
  38.6 3.2 %copy-start = (bf16[1024,4096]{1,0:T(8,128)(2,1)}, bf16[1024,4096]{1,0:T(8,128)(2,1)S(1)}, u32[]{:S(2)}) copy-start(bf16[1024,4096]{1,0:T(8,128)(2,1)S(1)} %counts.1) | copy-start | bytes 25165828
  77.4 34.2 %copy-start.4 = (f32[64]{0:T(128)S(1)}, f32[64]{0:T(128)}, u32[]{:S(2)}) copy-start(f32[64]{0:T(128)} %param.9) | copy-start | bytes 772
  77.4 34.7 %copy-start.3 = (f32[64,256]{1,0:T(8,128)S(1)}, f32[64,256]{1,0:T(8,128)}, u32[]{:S(2)}) copy-start(f32[64,256]{1,0:T(8,128)} %param.8) | copy-start | bytes 196612

commit v2 on v1

v2 whole, which is shorter than its diff:
```python
import jax
import jax.numpy as jnp
from jax import lax
from jax.experimental import pallas as pl
from jax.experimental.pallas import tpu as pltpu
from jax.sharding import Mesh, PartitionSpec as P

SLAB = 1024
STEP_RATE = 0.5
EPSILON = 1e-08
CORES = 2
VMEM = 56 * 1024 * 1024


def spread_kernel(grads_ref, out_ref):
    side = grads_ref.shape[0]
    features, width = grads_ref.shape[1:]
    half = width // CORES
    out_at = lax.broadcasted_iota(jnp.int32, (side * side, side * side), 0)
    in_at = lax.broadcasted_iota(jnp.int32, (side * side, side * side), 1)
    moved = (out_at % side) * side + out_at // side
    permutation = jnp.where(in_at == moved, 1.0, 0.0).astype(jnp.bfloat16)
    for first in range(0, features, side):
        block = grads_ref[:, first : first + side, :].reshape(side * side, width)
        turned = jnp.dot(permutation, block, preferred_element_type=jnp.float32)
        turned = turned.astype(jnp.bfloat16).reshape(side, side, width)
        for core in range(CORES):
            out_ref[first : first + side, core] = turned[:, :, core * half : (core + 1) * half]


def spread(grads):
    samples, features, width = grads.shape
    side = 16
    return pl.pallas_call(
        spread_kernel,
        grid=(samples // side,),
        in_specs=[pl.BlockSpec((side, features, width), lambda i: (i, 0, 0))],
        out_specs=pl.BlockSpec((features, CORES, side, width // CORES), lambda i: (0, 0, i, 0)),
        out_shape=jax.ShapeDtypeStruct((features, CORES, samples, width // CORES), grads.dtype),
        compiler_params=pltpu.CompilerParams(vmem_limit_bytes=VMEM),
        name="spread",
    )(grads)


def count_kernel(ids_ref, counts_ref):
    positions, width = ids_ref.shape[1:]
    slab = counts_ref.shape[1]
    tall = 64
    ids = [
        jnp.broadcast_to(ids_ref[0, p : p + 1, :], (tall, width)).astype(jnp.int16)
        for p in range(positions)
    ]
    row = lax.broadcasted_iota(jnp.int32, (tall, width), 0).astype(jnp.int16)
    one = jnp.ones((tall, width), jnp.bfloat16)
    zero = jnp.zeros((tall, width), jnp.bfloat16)

    def rows_block(i, carry):
        first = i * tall
        mine = row + first.astype(jnp.int16)
        total = zero
        for p in range(positions):
            total = total + jnp.where(ids[p] == mine, one, zero)
        counts_ref[0, pl.ds(pl.multiple_of(first, tall), tall), :] = total
        return carry

    lax.fori_loop(0, slab // tall, rows_block, 0)


def count_matrix(ids):
    cores, positions, samples = ids.shape
    width = 256
    return pl.pallas_call(
        count_kernel,
        grid=(cores, samples // width),
        in_specs=[pl.BlockSpec((1, positions, width), lambda c, i: (c, 0, i))],
        out_specs=pl.BlockSpec((1, SLAB, width), lambda c, i: (c, 0, i)),
        out_shape=jax.ShapeDtypeStruct((cores, SLAB, samples), jnp.bfloat16),
        compiler_params=pltpu.CompilerParams(vmem_limit_bytes=VMEM),
        cost_estimate=pl.CostEstimate(
            flops=16 * SLAB * samples * cores,
            bytes_accessed=2 * SLAB * samples * cores,
            transcendentals=0,
        ),
        name="counts",
    )(ids)


def pool_kernel(counts_ref, arrived_ref, out_ref, total_ref):
    step = pl.program_id(0)
    blocks, cores, depth, width = arrived_ref.shape

    @pl.when(step == 0)
    def _():
        total_ref[...] = jnp.zeros_like(total_ref)

    for core in range(cores):
        total_ref[...] += jnp.dot(
            counts_ref[core],
            arrived_ref[:, core].reshape(blocks * depth, width),
            preferred_element_type=jnp.float32,
        )

    @pl.when(step == pl.num_programs(0) - 1)
    def _():
        out_ref[...] = total_ref[...].astype(out_ref.dtype)


def pool(counts, arrived):
    blocks, cores, depth, width = arrived.shape
    at_once = 8
    return pl.pallas_call(
        pool_kernel,
        grid=(blocks // at_once,),
        in_specs=[
            pl.BlockSpec((cores, SLAB, at_once * depth), lambda i: (0, 0, i)),
            pl.BlockSpec((at_once, cores, depth, width), lambda i: (i, 0, 0, 0)),
        ],
        out_specs=pl.BlockSpec((SLAB, width), lambda i: (0, 0)),
        out_shape=jax.ShapeDtypeStruct((SLAB, width), jnp.bfloat16),
        scratch_shapes=[pltpu.VMEM((SLAB, width), jnp.float32)],
        compiler_params=pltpu.CompilerParams(vmem_limit_bytes=VMEM - 8 * 1024 * 1024),
        cost_estimate=pl.CostEstimate(
            flops=2 * SLAB * blocks * cores * depth * width,
            bytes_accessed=2 * SLAB * blocks * cores * depth,
            transcendentals=0,
        ),
        name="pool",
    )(counts, arrived)


def shards(grads, slots, lengths, rows, accum):
    _, mine, features, width = grads.shape
    positions, samples = slots.shape[2:]
    share = rows.shape[0]
    half = width // CORES
    outgoing = spread(grads.reshape(mine, features, width))
    arrived = lax.all_to_all(
        outgoing.reshape(features * CORES, mine, half), ("shard", "core"), 0, 0, tiled=True
    )
    place = lax.broadcasted_iota(jnp.int32, (positions, samples), 0)
    ids = jnp.where(place < lengths.reshape(1, samples), slots.reshape(positions, samples), -1)
    counts = count_matrix(lax.all_gather(ids, "core", axis=0, tiled=False))
    partial = pool(counts, arrived.reshape(features, CORES, mine, half))
    parts = lax.all_to_all(
        partial.reshape(SLAB // share, share, half), ("chip", "core"), 0, 0, tiled=True
    )
    halves = jnp.sum(
        parts.reshape(SLAB // share // CORES, CORES, share, half).astype(jnp.float32), axis=0
    )
    row_grad = jnp.concatenate([halves[core] for core in range(CORES)], axis=1)
    new_accum = accum + jnp.mean(row_grad * row_grad, axis=1)
    new_rows = rows - STEP_RATE * row_grad / (jnp.sqrt(new_accum)[:, None] + EPSILON)
    serving = lax.all_gather(
        new_rows.astype(jnp.bfloat16), ("chip", "core"), axis=0, tiled=True
    )
    return new_rows, new_accum, serving


def solution(mesh):
    shard, replica = mesh.devices.shape
    split = Mesh(
        mesh.devices.reshape(shard, replica // CORES, CORES), ("shard", "chip", "core")
    )
    replicas = ("chip", "core")
    owners = ("shard", "chip", "core")
    return jax.shard_map(
        shards,
        mesh=split,
        in_specs=(
            P(replicas, "shard", None, None),
            P(replicas, "shard", None, None),
            P(replicas, "shard", None),
            P(owners, None),
            P(owners),
        ),
        out_specs=(P(owners, None), P(owners), P("shard", None)),
        check_vma=False,
    )
```

time: 131 us -> 132 us (level)
  Pallas kernels: 9.72 us -> 38.8 us
  waiting for transfers between devices: 35.5 us -> 25.6 us
  local copies, waits for them, and re-layouts: 8.14 us -> 0.81 us
  blocking collectives: 44.1 us -> 37.5 us
  matrix products: 5.74 us -> 0 us
    pallas_call x1 -> x3, Pallas kernels: 9.72 us -> 38.8 us  [the longest x1 23.8 us: count_matrix(): pl.pallas_call(count_kernel, grid=(cores, samples // width), in_specs=[pl...]
    all_to_all x1, waiting for transfers between devices: 35.5 us -> 25.6 us  [shards(): lax.all_to_all(outgoing.reshape(features * CORES, mine, half), ('shard',...]
    all_to_all x1, blocking collectives: 28.3 us -> 18.9 us  [shards(): lax.all_to_all(partial.reshape(SLAB // share, share, half), ('chip', 'cor...]
    unnamed x12 -> x9, local copies, waits for them, and re-layouts: 8.14 us -> 0.81 us
    dot_general x1 -> x0, matrix products: 5.74 us -> none  [shards(): jnp.dot(counts, arrived.reshape(samples, width), preferred_element_type=j...]
    all_gather x1 -> x2, blocking collectives: 15.9 us -> 18.5 us  [the longest x1 15.9 us: shards(): lax.all_gather(new_rows.astype(jnp.bfloat16), ('chip', 'core'), axis=0, t...]
  transfers between devices with their start and end apart: 1 -> 1, of which waited for: 1 -> 1; matrix products, arithmetic and copies ran while one was open for 0% -> 0% of each run, Pallas kernels for 8% -> 18%
where the time goes in v2:
time: 132 us; the launch traced here: 130 us
  Pallas kernels  38.8 us (29%)
  blocking collectives  37.5 us (28%)
  waiting for transfers between devices  25.6 us (19%)
  starting transfers between devices  25.4 us (19%)
  other arithmetic  1.39 us (1%)
    all_to_all x1, waiting for transfers between devices, shards(): lax.all_to_all(outgoing.reshape(features * CORES, mine, half), ('shard',...  25.6 us
    all_to_all x1, starting transfers between devices, shards(): lax.all_to_all(outgoing.reshape(features * CORES, mine, half), ('shard',...  25.4 us
    pallas_call x1, Pallas kernels, count_matrix(): pl.pallas_call(count_kernel, grid=(cores, samples // width), in_specs=[pl...  23.8 us
    all_to_all x1, blocking collectives, shards(): lax.all_to_all(partial.reshape(SLAB // share, share, half), ('chip', 'cor...  18.9 us
    all_gather x1, blocking collectives, shards(): lax.all_gather(new_rows.astype(jnp.bfloat16), ('chip', 'core'), axis=0, t...  15.9 us
    pallas_call x1, Pallas kernels, pool(): pl.pallas_call(pool_kernel, grid=(blocks // at_once,), in_specs=[pl.Block...  10.5 us
    pallas_call x1, Pallas kernels, spread(): pl.pallas_call(spread_kernel, grid=(samples // side,), in_specs=[pl.Block...  4.42 us
    all_gather x1, blocking collectives, shards(): counts = count_matrix(lax.all_gather(ids, 'core', axis=0, tiled=False))  2.66 us
  transfers between devices with their start and end apart: 1, of which 1 were waited for; matrix products, arithmetic and copies ran while one was open for 0% of the time, Pallas kernels for 18%

profile of v2, /device:TPU:1, one launch (start us, length us, event | category | flops | bytes accessed | tf_op | source)
XLA Modules:
  0.0 130.1 jit_solution(15929310773638652650)
XLA Ops:
  0.6 4.4 %spread.1 = bf16[64,2,64,128]{3,2,1,0:T(8,128)(2,1)} custom-call(bf16[64,64,256]{2,1,0:T(8,128)(2,1)} %bitcast.16), custom_call_target="tpu_custom_call" | custom-call | tf_op jit(solution)/shard_map/spread/pallas_call | solution.py:34
  5.0 0.0 copy-start
  5.1 0.0 copy-start.2
  5.1 25.4 %all-to-all-start = ((bf16[128,64,128]{2,1,0:T(8,128)(2,1)}), bf16[128,64,128]{2,1,0:T(8,128)(2,1)S(1)}, u32[]{:S(2)}, u32[]{:S(2)}) async-start(bf16[128,64,128]{2,1,0:T(8,128)(2,1)} %bitcast.15), calls=%async_computation | async-start | bytes 4194304 | tf_op jit(solution)/shard_map/all_to_all | solution.py:137
  30.4 0.0 copy-done
  30.4 0.0 copy-done.2
  30.5 2.7 %all_gather.7.ids_ref = s32[2,8,4096]{2,1,0:T(8,128)} all-gather(s32[1,8,4096]{2,1,0:T(8,128)S(1)} %bitcast_select_fusion), channel_id=1, replica_groups=mesh['shard'=64,'chip'=8,'core'=2] {'core'}, dimensions={0}, use_global_device_ids=true | all-gather | bytes 393216 | tf_op jit(solution)/shard_map/all_gather | solution.py:142
  33.1 23.8 %counts.1.counts_ref = bf16[2,1024,4096]{2,1,0:T(8,128)(2,1)} custom-call(s32[2,8,4096]{2,1,0:T(8,128)} %all_gather.7.ids_ref), custom_call_target="tpu_custom_call" | custom-call | flops 134217728 | bytes 16777216 | tf_op jit(solution)/shard_map/counts/pallas_call | solution.py:72
  57.0 25.6 %all-to-all-done = bf16[128,64,128]{2,1,0:T(8,128)(2,1)S(1)} async-done(((bf16[128,64,128]{2,1,0:T(8,128)(2,1)}), bf16[128,64,128]{2,1,0:T(8,128)(2,1)S(1)}, u32[]{:S(2)}, u32[]{:S(2)}) %all-to-all-start) | async-done | bytes 2097184 | tf_op jit(solution)/shard_map/all_to_all | solution.py:137
  82.6 0.0 copy-start.3
  82.6 0.0 copy-start.1
  82.6 10.5 %pool.1 = bf16[1024,128]{1,0:T(8,128)(2,1)S(1)} custom-call(bf16[2,1024,4096]{2,1,0:T(8,128)(2,1)} %counts.1.counts_ref, bf16[64,2,64,128]{3,2,1,0:T(8,128)(2,1)S(1)} %bitcast.13), custom_call_target="tpu_custom_call" | custom-call | flops 2147483648 | bytes 16777216 | tf_op jit(solution)/shard_map/pool/pallas_call | solution.py:111
  93.1 18.9 %all_to_all.10 = bf16[16,64,128]{2,1,0:T(8,128)(2,1)S(1)} all-to-all(bf16[16,64,128]{2,1,0:T(8,128)(2,1)S(1)} %bitcast.14), channel_id=1, replica_groups=mesh['shard'=64,'chip'=8,'core'=2] {'chip','core'}, dimensions={0} | all-to-all | bytes 524288 | tf_op jit(solution)/shard_map/all_to_all | solution.py:144
  112.1 0.1 multiply_reduce_fusion
  112.2 0.0 copy-done.3
  112.2 0.5 sqrt_add_fusion
  112.7 0.0 copy-done.1
  112.7 0.7 fusion
  113.4 15.9 %all_gather.8 = bf16[1024,256]{1,0:T(8,128)(2,1)S(1)} all-gather(bf16[64,256]{1,0:T(8,128)(2,1)S(1)} %get-tuple-element.3), channel_id=1, replica_groups=mesh['shard'=64,'chip'=8,'core'=2] {'chip','core'}, dimensions={0}, use_global_device_ids=true | all-gather | bytes 557056 | tf_op jit(solution)/shard_map/all_gather | solution.py:153
  129.3 0.8 copy.9
  (3 shorter events, 0.1 us)
Async XLA Ops:
  5.0 25.4 %copy-start = (s32[1,1,8,4096]{3,2,1,0:T(8,128)S(1)}, s32[1,1,8,4096]{3,2,1,0:T(8,128)}, u32[]{:S(2)}) copy-start(s32[1,1,8,4096]{3,2,1,0:T(8,128)} %param.6) | copy-start | bytes 393220
  5.1 25.4 %copy-start.2 = (s32[1,1,4096]{2,1,0:T(1,128)S(1)}, s32[1,1,4096]{2,1,0:T(1,128)}, u32[]{:S(2)}) copy-start(s32[1,1,4096]{2,1,0:T(1,128)} %param.7) | copy-start | bytes 49156
  5.1 77.5 %all-to-all-start = ((bf16[128,64,128]{2,1,0:T(8,128)(2,1)}), bf16[128,64,128]{2,1,0:T(8,128)(2,1)S(1)}, u32[]{:S(2)}, u32[]{:S(2)}) async-start(bf16[128,64,128]{2,1,0:T(8,128)(2,1)} %bitcast.15), calls=%async_computation | async-start | bytes 4194304 | tf_op jit(solution)/shard_map/all_to_all | solution.py:137
  82.6 29.6 %copy-start.3 = (f32[64]{0:T(128)S(1)}, f32[64]{0:T(128)}, u32[]{:S(2)}) copy-start(f32[64]{0:T(128)} %param.9) | copy-start | bytes 772
  82.6 30.1 %copy-start.1 = (f32[64,256]{1,0:T(8,128)S(1)}, f32[64,256]{1,0:T(8,128)}, u32[]{:S(2)}) copy-start(f32[64,256]{1,0:T(8,128)} %param.8) | copy-start | bytes 196612

commit v3 on v2

v3 whole, which is shorter than its diff:
```python
import jax
import jax.numpy as jnp
from jax import lax
from jax.experimental import pallas as pl
from jax.experimental.pallas import tpu as pltpu
from jax.sharding import Mesh, PartitionSpec as P

SLAB = 1024
STEP_RATE = 0.5
EPSILON = 1e-08
CORES = 2
COUNT = jnp.float8_e4m3fn
VMEM = 56 * 1024 * 1024


def spread_kernel(grads_hbm, out_hbm, grads_ref, out_ref, in_sems, out_sems):
    samples, features, width = grads_ref.shape
    half = width // CORES
    side = features // in_sems.shape[0]
    reads, writes = [], []
    for i, first in enumerate(range(0, features, side)):
        mine = pl.ds(first, side)
        reads.append(
            pltpu.make_async_copy(grads_hbm.at[:, mine], grads_ref.at[:, mine], in_sems.at[i])
        )
        writes.append(pltpu.make_async_copy(out_ref.at[mine], out_hbm.at[mine], out_sems.at[i]))
    for read in reads:
        read.start()
    out_at = lax.broadcasted_iota(jnp.int32, (side * side, side * side), 0)
    in_at = lax.broadcasted_iota(jnp.int32, (side * side, side * side), 1)
    moved = (out_at % side) * side + out_at // side
    permutation = jnp.where(in_at == moved, 1.0, 0.0).astype(jnp.bfloat16)
    for i, first in enumerate(range(0, features, side)):
        reads[i].wait()
        for low in range(0, samples, side):
            block = grads_ref[low : low + side, first : first + side, :]
            turned = jnp.dot(
                permutation,
                block.reshape(side * side, width),
                preferred_element_type=jnp.float32,
            )
            turned = turned.astype(out_ref.dtype).reshape(side, side, width)
            for core in range(CORES):
                out_ref[first : first + side, core, low : low + side] = turned[
                    :, :, core * half : (core + 1) * half
                ]
        writes[i].start()
    for write in writes:
        write.wait()


def spread(grads):
    samples, features, width = grads.shape
    pieces = features // 16
    out = (features, CORES, samples, width // CORES)
    return pl.pallas_call(
        spread_kernel,
        in_specs=[pl.BlockSpec(memory_space=pl.ANY)],
        out_specs=pl.BlockSpec(memory_space=pl.ANY),
        out_shape=jax.ShapeDtypeStruct(out, grads.dtype),
        scratch_shapes=[
            pltpu.VMEM(grads.shape, grads.dtype),
            pltpu.VMEM(out, grads.dtype),
            pltpu.SemaphoreType.DMA((pieces,)),
            pltpu.SemaphoreType.DMA((pieces,)),
        ],
        compiler_params=pltpu.CompilerParams(vmem_limit_bytes=VMEM),
        name="spread",
    )(grads)


def count_kernel(ids_ref, counts_ref):
    positions = ids_ref.shape[1]
    blocks, _, depth, slab = counts_ref.shape
    tall, lanes = 32, 128
    ids = ids_ref[0].T
    lane = lax.broadcasted_iota(jnp.int32, (tall, lanes), 1).astype(jnp.int16)
    one = jnp.ones((tall, lanes), jnp.bfloat16)
    zero = jnp.zeros((tall, lanes), jnp.bfloat16)
    for block in range(blocks):
        for low in range(0, depth, tall):
            first = block * depth + low
            mine = [
                jnp.broadcast_to(ids[first : first + tall, p : p + 1], (tall, lanes)).astype(
                    jnp.int16
                )
                for p in range(positions)
            ]
            for left in range(0, slab, lanes):
                here = lane + jnp.int16(left)
                total = zero
                for p in range(positions):
                    total = total + jnp.where(mine[p] == here, one, zero)
                counts_ref[block, 0, low : low + tall, left : left + lanes] = total.astype(
                    counts_ref.dtype
                )


def count_matrix(ids, depth):
    cores, positions, samples = ids.shape
    blocks = 4
    return pl.pallas_call(
        count_kernel,
        grid=(cores, samples // (blocks * depth)),
        in_specs=[pl.BlockSpec((1, positions, blocks * depth), lambda c, i: (c, 0, i))],
        out_specs=pl.BlockSpec((blocks, 1, depth, SLAB), lambda c, i: (i, c, 0, 0)),
        out_shape=jax.ShapeDtypeStruct((samples // depth, cores, depth, SLAB), COUNT),
        compiler_params=pltpu.CompilerParams(vmem_limit_bytes=VMEM),
        cost_estimate=pl.CostEstimate(
            flops=16 * SLAB * samples * cores,
            bytes_accessed=SLAB * samples * cores,
            transcendentals=0,
        ),
        name="counts",
    )(ids)


def pool_kernel(counts_hbm, arrived_hbm, out_ref, counts_ref, arrived_ref, total_ref, sems):
    pieces = counts_ref.shape[0]
    depth = counts_ref.shape[1]

    def fetch(i):
        return (
            pltpu.make_async_copy(
                counts_hbm.at[pl.ds(i * depth, depth)], counts_ref.at[i], sems.at[0, i]
            ),
            pltpu.make_async_copy(
                arrived_hbm.at[pl.ds(i * depth, depth)], arrived_ref.at[i], sems.at[1, i]
            ),
        )

    copies = [fetch(i) for i in range(pieces)]
    for pair in copies:
        for copy in pair:
            copy.start()
    for i, pair in enumerate(copies):
        for copy in pair:
            copy.wait()
        product = lax.dot_general(
            arrived_ref[i],
            counts_ref[i].astype(jnp.bfloat16),
            (((0,), (0,)), ((), ())),
            preferred_element_type=jnp.float32,
        )
        if i == 0:
            total_ref[...] = product
        elif i < pieces - 1:
            total_ref[...] += product
        else:
            out_ref[...] = (total_ref[...] + product).T.astype(out_ref.dtype)


def pool(counts, arrived, pieces=8):
    samples, width = arrived.shape
    slab = counts.shape[1]
    depth = samples // pieces
    return pl.pallas_call(
        pool_kernel,
        in_specs=[pl.BlockSpec(memory_space=pl.ANY)] * 2,
        out_specs=pl.BlockSpec(memory_space=pltpu.VMEM),
        out_shape=jax.ShapeDtypeStruct((slab, width), jnp.bfloat16),
        scratch_shapes=[
            pltpu.VMEM((pieces, depth, slab), counts.dtype),
            pltpu.VMEM((pieces, depth, width), arrived.dtype),
            pltpu.VMEM((width, slab), jnp.float32),
            pltpu.SemaphoreType.DMA((2, pieces)),
        ],
        compiler_params=pltpu.CompilerParams(vmem_limit_bytes=VMEM - 8 * 1024 * 1024),
        cost_estimate=pl.CostEstimate(
            flops=2 * slab * samples * width,
            bytes_accessed=slab * samples,
            transcendentals=0,
        ),
        name="pool",
    )(counts, arrived)


def shards(grads, slots, lengths, rows, accum):
    _, mine, features, width = grads.shape
    positions, samples = slots.shape[2:]
    share = rows.shape[0]
    half = width // CORES
    outgoing = spread(grads.reshape(mine, features, width))
    arrived = lax.all_to_all(
        outgoing.reshape(features * CORES, mine, half), ("shard", "core"), 0, 0, tiled=True
    )
    place = lax.broadcasted_iota(jnp.int32, (positions, samples), 0)
    ids = jnp.where(place < lengths.reshape(1, samples), slots.reshape(positions, samples), -1)
    counts = count_matrix(lax.all_gather(ids, "core", axis=0, tiled=False), mine)
    partial = pool(
        counts.reshape(CORES * samples, SLAB), arrived.reshape(CORES * samples, half)
    )
    parts = lax.all_to_all(
        partial.reshape(SLAB // share, share, half), ("chip", "core"), 0, 0, tiled=True
    )
    halves = jnp.sum(
        parts.reshape(SLAB // share // CORES, CORES, share, half).astype(jnp.float32), axis=0
    )
    row_grad = jnp.concatenate([halves[core] for core in range(CORES)], axis=1)
    new_accum = accum + jnp.mean(row_grad * row_grad, axis=1)
    new_rows = rows - STEP_RATE * row_grad / (jnp.sqrt(new_accum)[:, None] + EPSILON)
    serving = lax.all_gather(
        new_rows.astype(jnp.bfloat16), ("chip", "core"), axis=0, tiled=True
    )
    return new_rows, new_accum, serving


def solution(mesh):
    shard, replica = mesh.devices.shape
    split = Mesh(
        mesh.devices.reshape(shard, replica // CORES, CORES), ("shard", "chip", "core")
    )
    replicas = ("chip", "core")
    owners = ("shard", "chip", "core")
    return jax.shard_map(
        shards,
        mesh=split,
        in_specs=(
            P(replicas, "shard", None, None),
            P(replicas, "shard", None, None),
            P(replicas, "shard", None),
            P(owners, None),
            P(owners),
        ),
        out_specs=(P(owners, None), P(owners), P("shard", None)),
        check_vma=False,
    )
```

time: 132 us -> 125 us (0.947)
  Pallas kernels: 38.8 us -> 31.5 us
    pallas_call x3, Pallas kernels: 38.8 us -> 31.5 us  [the longest x1 24 us: count_matrix(): pl.pallas_call(count_kernel, grid=(cores, samples // (blocks * depth)), i...]
  transfers between devices with their start and end apart: 1 -> 1, of which waited for: 1 -> 1; matrix products, arithmetic and copies ran while one was open for 0% -> 0% of each run, Pallas kernels for 18% -> 20%
where the time goes in v3:
time: 125 us; the launch traced here: 123 us
  blocking collectives  37.5 us (30%)
  Pallas kernels  31.5 us (25%)
  waiting for transfers between devices  25.5 us (20%)
  starting transfers between devices  25.4 us (20%)
  other arithmetic  1.39 us (1%)
    all_to_all x1, waiting for transfers between devices, shards(): lax.all_to_all(outgoing.reshape(features * CORES, mine, half), ('shard',...  25.5 us
    all_to_all x1, starting transfers between devices, shards(): lax.all_to_all(outgoing.reshape(features * CORES, mine, half), ('shard',...  25.4 us
    pallas_call x1, Pallas kernels, count_matrix(): pl.pallas_call(count_kernel, grid=(cores, samples // (blocks * depth)), i...  24 us
    all_to_all x1, blocking collectives, shards(): lax.all_to_all(partial.reshape(SLAB // share, share, half), ('chip', 'cor...  18.9 us
    all_gather x1, blocking collectives, shards(): lax.all_gather(new_rows.astype(jnp.bfloat16), ('chip', 'core'), axis=0, t...  15.9 us
    pallas_call x1, Pallas kernels, pool(): pl.pallas_call(pool_kernel, in_specs=[pl.BlockSpec(memory_space=pl.ANY)]...  4.42 us
    pallas_call x1, Pallas kernels, spread(): pl.pallas_call(spread_kernel, in_specs=[pl.BlockSpec(memory_space=pl.ANY)...  3.11 us
    all_gather x1, blocking collectives, shards(): lax.all_gather(ids, 'core', axis=0, tiled=False)  2.66 us
  transfers between devices with their start and end apart: 1, of which 1 were waited for; matrix products, arithmetic and copies ran while one was open for 0% of the time, Pallas kernels for 20%

profile of v3, /device:TPU:1, one launch (start us, length us, event | category | flops | bytes accessed | tf_op | source)
XLA Modules:
  0.0 122.7 jit_solution(3595654579709417006)
XLA Ops:
  0.6 3.1 %spread.1 = bf16[64,2,64,128]{3,2,1,0:T(8,128)(2,1)} custom-call(bf16[64,64,256]{2,1,0:T(8,128)(2,1)} %bitcast.18), custom_call_target="tpu_custom_call" | custom-call | tf_op jit(solution)/shard_map/spread/pallas_call | solution.py:56
  3.7 0.0 copy-start
  3.8 0.0 copy-start.2
  3.8 25.4 %all-to-all-start = ((bf16[128,64,128]{2,1,0:T(8,128)(2,1)}), bf16[128,64,128]{2,1,0:T(8,128)(2,1)S(1)}, u32[]{:S(2)}, u32[]{:S(2)}) async-start(bf16[128,64,128]{2,1,0:T(8,128)(2,1)} %bitcast.17), calls=%async_computation | async-start | bytes 4194304 | tf_op jit(solution)/shard_map/all_to_all | solution.py:184
  29.2 0.0 copy-done
  29.2 0.0 copy-done.2
  29.2 2.7 %all_gather.7.ids_ref = s32[2,8,4096]{2,1,0:T(8,128)} all-gather(s32[1,8,4096]{2,1,0:T(8,128)S(1)} %bitcast_select_fusion), channel_id=1, replica_groups=mesh['shard'=64,'chip'=8,'core'=2] {'core'}, dimensions={0}, use_global_device_ids=true | all-gather | bytes 393216 | tf_op jit(solution)/shard_map/all_gather | solution.py:189
  31.9 24.0 %counts.1 = f8e4m3fn[64,2,64,1024]{3,2,1,0:T(32,128)(4,1)} custom-call(s32[2,8,4096]{2,1,0:T(8,128)} %all_gather.7.ids_ref), custom_call_target="tpu_custom_call" | custom-call | flops 134217728 | bytes 8388608 | tf_op jit(solution)/shard_map/counts/pallas_call | solution.py:102
  55.8 25.5 %all-to-all-done = bf16[128,64,128]{2,1,0:T(8,128)(2,1)S(1)} async-done(((bf16[128,64,128]{2,1,0:T(8,128)(2,1)}), bf16[128,64,128]{2,1,0:T(8,128)(2,1)S(1)}, u32[]{:S(2)}, u32[]{:S(2)}) %all-to-all-start) | async-done | bytes 2097184 | tf_op jit(solution)/shard_map/all_to_all | solution.py:184
  81.3 0.0 copy-start.3
  81.3 0.0 copy-start.1
  81.3 4.4 %pool.1 = bf16[1024,128]{1,0:T(8,128)(2,1)S(1)} custom-call(f8e4m3fn[8192,1024]{1,0:T(32,128)(4,1)} %bitcast.16, bf16[8192,128]{1,0:T(8,128)(2,1)S(1)} %bitcast.14), custom_call_target="tpu_custom_call" | custom-call | flops 2147483648 | bytes 8388608 | tf_op jit(solution)/shard_map/pool/pallas_call | solution.py:157
  85.7 18.9 %all_to_all.10 = bf16[16,64,128]{2,1,0:T(8,128)(2,1)S(1)} all-to-all(bf16[16,64,128]{2,1,0:T(8,128)(2,1)S(1)} %bitcast.15), channel_id=1, replica_groups=mesh['shard'=64,'chip'=8,'core'=2] {'chip','core'}, dimensions={0} | all-to-all | bytes 524288 | tf_op jit(solution)/shard_map/all_to_all | solution.py:193
  104.7 0.1 multiply_reduce_fusion
  104.8 0.0 copy-done.3
  104.8 0.5 sqrt_add_fusion
  105.3 0.0 copy-done.1
  105.3 0.7 fusion
  106.1 15.9 %all_gather.8 = bf16[1024,256]{1,0:T(8,128)(2,1)S(1)} all-gather(bf16[64,256]{1,0:T(8,128)(2,1)S(1)} %get-tuple-element.3), channel_id=1, replica_groups=mesh['shard'=64,'chip'=8,'core'=2] {'chip','core'}, dimensions={0}, use_global_device_ids=true | all-gather | bytes 557056 | tf_op jit(solution)/shard_map/all_gather | solution.py:202
  121.9 0.8 copy.9
  (3 shorter events, 0.1 us)
Async XLA Ops:
  3.7 25.4 %copy-start = (s32[1,1,8,4096]{3,2,1,0:T(8,128)S(1)}, s32[1,1,8,4096]{3,2,1,0:T(8,128)}, u32[]{:S(2)}) copy-start(s32[1,1,8,4096]{3,2,1,0:T(8,128)} %param.6) | copy-start | bytes 393220
  3.8 25.4 %copy-start.2 = (s32[1,1,4096]{2,1,0:T(1,128)S(1)}, s32[1,1,4096]{2,1,0:T(1,128)}, u32[]{:S(2)}) copy-start(s32[1,1,4096]{2,1,0:T(1,128)} %param.7) | copy-start | bytes 49156
  3.8 77.5 %all-to-all-start = ((bf16[128,64,128]{2,1,0:T(8,128)(2,1)}), bf16[128,64,128]{2,1,0:T(8,128)(2,1)S(1)}, u32[]{:S(2)}, u32[]{:S(2)}) async-start(bf16[128,64,128]{2,1,0:T(8,128)(2,1)} %bitcast.17), calls=%async_computation | async-start | bytes 4194304 | tf_op jit(solution)/shard_map/all_to_all | solution.py:184
  81.3 23.5 %copy-start.3 = (f32[64]{0:T(128)S(1)}, f32[64]{0:T(128)}, u32[]{:S(2)}) copy-start(f32[64]{0:T(128)} %param.9) | copy-start | bytes 772
  81.3 24.0 %copy-start.1 = (f32[64,256]{1,0:T(8,128)S(1)}, f32[64,256]{1,0:T(8,128)}, u32[]{:S(2)}) copy-start(f32[64,256]{1,0:T(8,128)} %param.8) | copy-start | bytes 196612

commit v4 on v3

--- a/solution.py
+++ b/solution.py
@@ -147,10 +147,15 @@
         elif i < pieces - 1:
             total_ref[...] += product
         else:
-            out_ref[...] = (total_ref[...] + product).T.astype(out_ref.dtype)
-
-
-def pool(counts, arrived, pieces=8):
+            pooled = (total_ref[...] + product).T.astype(out_ref.dtype)
+            cores, chips, share, _ = out_ref.shape
+            for core in range(cores):
+                for chip in range(chips):
+                    first = (chip * cores + core) * share
+                    out_ref[core, chip] = pooled[first : first + share]
+
+
+def pool(counts, arrived, share, pieces=8):
     samples, width = arrived.shape
     slab = counts.shape[1]
     depth = samples // pieces
@@ -158,7 +163,9 @@
         pool_kernel,
         in_specs=[pl.BlockSpec(memory_space=pl.ANY)] * 2,
         out_specs=pl.BlockSpec(memory_space=pltpu.VMEM),
-        out_shape=jax.ShapeDtypeStruct((slab, width), jnp.bfloat16),
+        out_shape=jax.ShapeDtypeStruct(
+            (CORES, slab // share // CORES, share, width), jnp.bfloat16
+        ),
         scratch_shapes=[
             pltpu.VMEM((pieces, depth, slab), counts.dtype),
             pltpu.VMEM((pieces, depth, width), arrived.dtype),
@@ -175,6 +182,43 @@
     )(counts, arrived)
 
 
+def update_kernel(parts_ref, rows_ref, accum_ref, new_rows_ref, new_accum_ref, serving_ref):
+    cores, chips, _, half = parts_ref.shape
+    halves = []
+    for core in range(cores):
+        total = parts_ref[core, 0].astype(jnp.float32)
+        for chip in range(1, chips):
+            total = total + parts_ref[core, chip].astype(jnp.float32)
+        halves.append(total)
+    square = halves[0] * halves[0]
+    for total in halves[1:]:
+        square = square + total * total
+    mean = jnp.sum(square, axis=1, keepdims=True) / (cores * half)
+    accum = accum_ref[...].T + mean
+    new_accum_ref[...] = accum.T
+    scale = STEP_RATE / (jnp.sqrt(accum) + EPSILON)
+    for core, total in enumerate(halves):
+        mine = slice(core * half, (core + 1) * half)
+        fresh = rows_ref[:, mine] - total * scale
+        new_rows_ref[:, mine] = fresh
+        serving_ref[:, mine] = fresh.astype(serving_ref.dtype)
+
+
+def update(parts, rows, accum):
+    share = rows.shape[0]
+    new_rows, new_accum, serving = pl.pallas_call(
+        update_kernel,
+        out_shape=(
+            jax.ShapeDtypeStruct(rows.shape, rows.dtype),
+            jax.ShapeDtypeStruct((1, share), accum.dtype),
+            jax.ShapeDtypeStruct(rows.shape, jnp.bfloat16),
+        ),
+        compiler_params=pltpu.CompilerParams(vmem_limit_bytes=8 * 1024 * 1024),
+        name="update",
+    )(parts, rows, accum.reshape(1, share))
+    return new_rows, new_accum.reshape(share), serving
+
+
 def shards(grads, slots, lengths, rows, accum):
     _, mine, features, width = grads.shape
     positions, samples = slots.shape[2:]
@@ -188,20 +232,15 @@
     ids = jnp.where(place < lengths.reshape(1, samples), slots.reshape(positions, samples), -1)
     counts = count_matrix(lax.all_gather(ids, "core", axis=0, tiled=False), mine)
     partial = pool(
-        counts.reshape(CORES * samples, SLAB), arrived.reshape(CORES * samples, half)
+        counts.reshape(CORES * samples, SLAB), arrived.reshape(CORES * samples, half), share
     )
     parts = lax.all_to_all(
-        partial.reshape(SLAB // share, share, half), ("chip", "core"), 0, 0, tiled=True
-    )
-    halves = jnp.sum(
-        parts.reshape(SLAB // share // CORES, CORES, share, half).astype(jnp.float32), axis=0
-    )
-    row_grad = jnp.concatenate([halves[core] for core in range(CORES)], axis=1)
-    new_accum = accum + jnp.mean(row_grad * row_grad, axis=1)
-    new_rows = rows - STEP_RATE * row_grad / (jnp.sqrt(new_accum)[:, None] + EPSILON)
-    serving = lax.all_gather(
-        new_rows.astype(jnp.bfloat16), ("chip", "core"), axis=0, tiled=True
-    )
+        partial.reshape(SLAB // share, share, half), ("core", "chip"), 0, 0, tiled=True
+    )
+    new_rows, new_accum, fresh = update(
+        parts.reshape(CORES, SLAB // share // CORES, share, half), rows, accum
+    )
+    serving = lax.all_gather(fresh, ("chip", "core"), axis=0, tiled=True)
     return new_rows, new_accum, serving
 
 

time: 125 us -> 125 us (level)
  other arithmetic: 1.39 us -> 0.02 us
    all_gather x1, blocking collectives: 15.9 us -> 18.9 us  [shards(): serving = lax.all_gather(fresh, ('chip', 'core'), axis=0, tiled=True)]
    all_to_all x1, blocking collectives: 18.9 us -> 16.6 us  [shards(): lax.all_to_all(partial.reshape(SLAB // share, share, half), ('core', 'chi...]
where the time goes in v4:
time: 125 us; the launch traced here: 123 us
  blocking collectives  38.2 us (31%)
  Pallas kernels  32.4 us (26%)
  waiting for transfers between devices  25.5 us (20%)
  starting transfers between devices  25.4 us (20%)
    all_to_all x1, waiting for transfers between devices, shards(): lax.all_to_all(outgoing.reshape(features * CORES, mine, half), ('shard',...  25.5 us
    all_to_all x1, starting transfers between devices, shards(): lax.all_to_all(outgoing.reshape(features * CORES, mine, half), ('shard',...  25.4 us
    pallas_call x1, Pallas kernels, count_matrix(): pl.pallas_call(count_kernel, grid=(cores, samples // (blocks * depth)), i...  24 us
    all_gather x1, blocking collectives, shards(): serving = lax.all_gather(fresh, ('chip', 'core'), axis=0, tiled=True)  18.9 us
    all_to_all x1, blocking collectives, shards(): lax.all_to_all(partial.reshape(SLAB // share, share, half), ('core', 'chi...  16.6 us
    pallas_call x1, Pallas kernels, pool(): pl.pallas_call(pool_kernel, in_specs=[pl.BlockSpec(memory_space=pl.ANY)]...  4.43 us
    pallas_call x1, Pallas kernels, spread(): pl.pallas_call(spread_kernel, in_specs=[pl.BlockSpec(memory_space=pl.ANY)...  3.11 us
    all_gather x1, blocking collectives, shards(): lax.all_gather(ids, 'core', axis=0, tiled=False)  2.66 us
  transfers between devices with their start and end apart: 1, of which 1 were waited for; matrix products, arithmetic and copies ran while one was open for 0% of the time, Pallas kernels for 20%

profile of v4, /device:TPU:1, one launch (start us, length us, event | category | flops | bytes accessed | tf_op | source)
XLA Modules:
  0.0 122.9 jit_solution(15394285814238298028)
XLA Ops:
  0.6 3.1 %spread.1 = bf16[64,2,64,128]{3,2,1,0:T(8,128)(2,1)} custom-call(bf16[64,64,256]{2,1,0:T(8,128)(2,1)} %bitcast.17), custom_call_target="tpu_custom_call" | custom-call | tf_op jit(solution)/shard_map/spread/pallas_call | solution.py:56
  3.7 0.0 copy-start.2
  3.8 0.0 copy-start.3
  3.8 25.4 %all-to-all-start = ((bf16[128,64,128]{2,1,0:T(8,128)(2,1)}), bf16[128,64,128]{2,1,0:T(8,128)(2,1)S(1)}, u32[]{:S(2)}, u32[]{:S(2)}) async-start(bf16[128,64,128]{2,1,0:T(8,128)(2,1)} %bitcast.16), calls=%async_computation | async-start | bytes 4194304 | tf_op jit(solution)/shard_map/all_to_all | solution.py:228
  29.2 0.0 copy-done.2
  29.2 0.0 copy-done.3
  29.2 2.7 %all_gather.7.ids_ref = s32[2,8,4096]{2,1,0:T(8,128)} all-gather(s32[1,8,4096]{2,1,0:T(8,128)S(1)} %bitcast_select_fusion), channel_id=1, replica_groups=mesh['shard'=64,'chip'=8,'core'=2] {'core'}, dimensions={0}, use_global_device_ids=true | all-gather | bytes 393216 | tf_op jit(solution)/shard_map/all_gather | solution.py:233
  31.9 24.0 %counts.1 = f8e4m3fn[64,2,64,1024]{3,2,1,0:T(32,128)(4,1)} custom-call(s32[2,8,4096]{2,1,0:T(8,128)} %all_gather.7.ids_ref), custom_call_target="tpu_custom_call" | custom-call | flops 134217728 | bytes 8388608 | tf_op jit(solution)/shard_map/counts/pallas_call | solution.py:102
  55.8 25.5 %all-to-all-done = bf16[128,64,128]{2,1,0:T(8,128)(2,1)S(1)} async-done(((bf16[128,64,128]{2,1,0:T(8,128)(2,1)}), bf16[128,64,128]{2,1,0:T(8,128)(2,1)S(1)}, u32[]{:S(2)}, u32[]{:S(2)}) %all-to-all-start) | async-done | bytes 2097184 | tf_op jit(solution)/shard_map/all_to_all | solution.py:228
  81.3 0.0 copy-start
  81.3 0.0 copy-start.1
  81.3 4.4 %pool.1 = bf16[2,8,64,128]{3,2,1,0:T(8,128)(2,1)S(1)} custom-call(f8e4m3fn[8192,1024]{1,0:T(32,128)(4,1)} %bitcast.15, bf16[8192,128]{1,0:T(8,128)(2,1)S(1)} %bitcast.11), custom_call_target="tpu_custom_call" | custom-call | flops 2147483648 | bytes 8388608 | tf_op jit(solution)/shard_map/pool/pallas_call | solution.py:162
  85.7 16.6 %all_to_all.10 = bf16[16,64,128]{2,1,0:T(8,128)(2,1)S(1)} all-to-all(bf16[16,64,128]{2,1,0:T(8,128)(2,1)S(1)} %bitcast.13), channel_id=1, replica_groups=mesh['shard'=64,'chip'=8,'core'=2] {'core','chip'}, dimensions={0} | all-to-all | bytes 524288 | tf_op jit(solution)/shard_map/all_to_all | solution.py:237
  102.3 0.0 copy-done
  102.3 0.0 copy-done.1
  102.3 0.9 update.1
  103.2 18.9 %all_gather.8 = bf16[1024,256]{1,0:T(8,128)(2,1)S(1)} all-gather(bf16[64,256]{1,0:T(8,128)(2,1)S(1)} %get-tuple-element.8), channel_id=1, replica_groups=mesh['shard'=64,'chip'=8,'core'=2] {'chip','core'}, dimensions={0}, use_global_device_ids=true | all-gather | bytes 557056 | tf_op jit(solution)/shard_map/all_gather | solution.py:243
  122.2 0.8 copy.9
  (1 shorter events, 0.0 us)
Async XLA Ops:
  3.7 25.4 %copy-start.2 = (s32[1,1,8,4096]{3,2,1,0:T(8,128)S(1)}, s32[1,1,8,4096]{3,2,1,0:T(8,128)}, u32[]{:S(2)}) copy-start(s32[1,1,8,4096]{3,2,1,0:T(8,128)} %param.6) | copy-start | bytes 393220
  3.8 25.4 %copy-start.3 = (s32[1,1,4096]{2,1,0:T(1,128)S(1)}, s32[1,1,4096]{2,1,0:T(1,128)}, u32[]{:S(2)}) copy-start(s32[1,1,4096]{2,1,0:T(1,128)} %param.7) | copy-start | bytes 49156
  3.8 77.5 %all-to-all-start = ((bf16[128,64,128]{2,1,0:T(8,128)(2,1)}), bf16[128,64,128]{2,1,0:T(8,128)(2,1)S(1)}, u32[]{:S(2)}, u32[]{:S(2)}) async-start(bf16[128,64,128]{2,1,0:T(8,128)(2,1)} %bitcast.16), calls=%async_computation | async-start | bytes 4194304 | tf_op jit(solution)/shard_map/all_to_all | solution.py:228
  81.3 21.0 %copy-start = (f32[64,256]{1,0:T(8,128)S(1)}, f32[64,256]{1,0:T(8,128)}, u32[]{:S(2)}) copy-start(f32[64,256]{1,0:T(8,128)} %rows_ref.1) | copy-start | bytes 196612
  81.3 21.0 %copy-start.1 = (f32[64]{0:T(128)S(1)}, f32[64]{0:T(128)}, u32[]{:S(2)}) copy-start(f32[64]{0:T(128)} %param.9) | copy-start | bytes 772

commit v5 on v4

--- a/solution.py
+++ b/solution.py
@@ -26,20 +26,11 @@
         writes.append(pltpu.make_async_copy(out_ref.at[mine], out_hbm.at[mine], out_sems.at[i]))
     for read in reads:
         read.start()
-    out_at = lax.broadcasted_iota(jnp.int32, (side * side, side * side), 0)
-    in_at = lax.broadcasted_iota(jnp.int32, (side * side, side * side), 1)
-    moved = (out_at % side) * side + out_at // side
-    permutation = jnp.where(in_at == moved, 1.0, 0.0).astype(jnp.bfloat16)
     for i, first in enumerate(range(0, features, side)):
         reads[i].wait()
         for low in range(0, samples, side):
             block = grads_ref[low : low + side, first : first + side, :]
-            turned = jnp.dot(
-                permutation,
-                block.reshape(side * side, width),
-                preferred_element_type=jnp.float32,
-            )
-            turned = turned.astype(out_ref.dtype).reshape(side, side, width)
+            turned = jnp.swapaxes(block, 0, 1)
             for core in range(CORES):
                 out_ref[first : first + side, core, low : low + side] = turned[
                     :, :, core * half : (core + 1) * half
@@ -201,7 +192,8 @@
         mine = slice(core * half, (core + 1) * half)
         fresh = rows_ref[:, mine] - total * scale
         new_rows_ref[:, mine] = fresh
-        serving_ref[:, mine] = fresh.astype(serving_ref.dtype)
+        for chip in range(chips):
+            serving_ref[chip, :, mine] = fresh.astype(serving_ref.dtype)
 
 
 def update(parts, rows, accum):
@@ -211,7 +203,7 @@
         out_shape=(
             jax.ShapeDtypeStruct(rows.shape, rows.dtype),
             jax.ShapeDtypeStruct((1, share), accum.dtype),
-            jax.ShapeDtypeStruct(rows.shape, jnp.bfloat16),
+            jax.ShapeDtypeStruct((parts.shape[1],) + rows.shape, jnp.bfloat16),
         ),
         compiler_params=pltpu.CompilerParams(vmem_limit_bytes=8 * 1024 * 1024),
         name="update",
@@ -240,7 +232,9 @@
     new_rows, new_accum, fresh = update(
         parts.reshape(CORES, SLAB // share // CORES, share, half), rows, accum
     )
-    serving = lax.all_gather(fresh, ("chip", "core"), axis=0, tiled=True)
+    alike = lax.all_to_all(fresh, "chip", 0, 0, tiled=True)
+    pairs = lax.all_gather(alike, "core", axis=0, tiled=False)
+    serving = pairs.transpose(1, 0, 2, 3).reshape(SLAB, width)
     return new_rows, new_accum, serving
 
 

time: 125 us -> 124 us (level)
    all_gather x1, blocking collectives: 18.9 us -> 3.93 us  [shards(): pairs = lax.all_gather(alike, 'core', axis=0, tiled=False)]
    all_to_all x0 -> x1, blocking collectives: none -> 14.9 us  [shards(): alike = lax.all_to_all(fresh, 'chip', 0, 0, tiled=True)]
where the time goes in v5:
time: 124 us; the launch traced here: 122 us
  blocking collectives  38.1 us (31%)
  Pallas kernels  31.9 us (26%)
  waiting for transfers between devices  25.5 us (21%)
  starting transfers between devices  25.4 us (20%)
    all_to_all x1, waiting for transfers between devices, shards(): lax.all_to_all(outgoing.reshape(features * CORES, mine, half), ('shard',...  25.5 us
    all_to_all x1, starting transfers between devices, shards(): lax.all_to_all(outgoing.reshape(features * CORES, mine, half), ('shard',...  25.4 us
    pallas_call x1, Pallas kernels, count_matrix(): pl.pallas_call(count_kernel, grid=(cores, samples // (blocks * depth)), i...  24 us
    all_to_all x1, blocking collectives, shards(): lax.all_to_all(partial.reshape(SLAB // share, share, half), ('core', 'chi...  16.6 us
    all_to_all x1, blocking collectives, shards(): alike = lax.all_to_all(fresh, 'chip', 0, 0, tiled=True)  14.9 us
    pallas_call x1, Pallas kernels, pool(): pl.pallas_call(pool_kernel, in_specs=[pl.BlockSpec(memory_space=pl.ANY)]...  4.4 us
    all_gather x1, blocking collectives, shards(): pairs = lax.all_gather(alike, 'core', axis=0, tiled=False)  3.93 us
    all_gather x1, blocking collectives, shards(): lax.all_gather(ids, 'core', axis=0, tiled=False)  2.66 us
  transfers between devices with their start and end apart: 1, of which 1 were waited for; matrix products, arithmetic and copies ran while one was open for 0% of the time, Pallas kernels for 20%

profile of v5, /device:TPU:1, one launch (start us, length us, event | category | flops | bytes accessed | tf_op | source)
XLA Modules:
  0.0 122.4 jit_solution(4366207397467459976)
XLA Ops:
  0.6 2.6 %spread.1 = bf16[64,2,64,128]{3,2,1,0:T(8,128)(2,1)} custom-call(bf16[64,64,256]{2,1,0:T(8,128)(2,1)} %bitcast.21), custom_call_target="tpu_custom_call" | custom-call | tf_op jit(solution)/shard_map/spread/pallas_call | solution.py:47
  3.3 0.0 copy-start.2
  3.3 0.0 copy-start.3
  3.3 25.4 %all-to-all-start = ((bf16[128,64,128]{2,1,0:T(8,128)(2,1)}), bf16[128,64,128]{2,1,0:T(8,128)(2,1)S(1)}, u32[]{:S(2)}, u32[]{:S(2)}) async-start(bf16[128,64,128]{2,1,0:T(8,128)(2,1)} %bitcast.20), calls=%async_computation | async-start | bytes 4194304 | tf_op jit(solution)/shard_map/all_to_all | solution.py:220
  28.7 0.0 copy-done.2
  28.7 0.0 copy-done.3
  28.7 2.7 %all_gather.10.ids_ref = s32[2,8,4096]{2,1,0:T(8,128)} all-gather(s32[1,8,4096]{2,1,0:T(8,128)S(1)} %bitcast_select_fusion), channel_id=1, replica_groups=mesh['shard'=64,'chip'=8,'core'=2] {'core'}, dimensions={0}, use_global_device_ids=true | all-gather | bytes 393216 | tf_op jit(solution)/shard_map/all_gather | solution.py:225
  31.4 24.0 %counts.1 = f8e4m3fn[64,2,64,1024]{3,2,1,0:T(32,128)(4,1)} custom-call(s32[2,8,4096]{2,1,0:T(8,128)} %all_gather.10.ids_ref), custom_call_target="tpu_custom_call" | custom-call | flops 134217728 | bytes 8388608 | tf_op jit(solution)/shard_map/counts/pallas_call | solution.py:93
  55.4 25.5 %all-to-all-done = bf16[128,64,128]{2,1,0:T(8,128)(2,1)S(1)} async-done(((bf16[128,64,128]{2,1,0:T(8,128)(2,1)}), bf16[128,64,128]{2,1,0:T(8,128)(2,1)S(1)}, u32[]{:S(2)}, u32[]{:S(2)}) %all-to-all-start) | async-done | bytes 2097184 | tf_op jit(solution)/shard_map/all_to_all | solution.py:220
  80.8 0.0 copy-start
  80.8 0.0 copy-start.1
  80.8 4.4 %pool.1 = bf16[2,8,64,128]{3,2,1,0:T(8,128)(2,1)S(1)} custom-call(f8e4m3fn[8192,1024]{1,0:T(32,128)(4,1)} %bitcast.19, bf16[8192,128]{1,0:T(8,128)(2,1)S(1)} %bitcast.15), custom_call_target="tpu_custom_call" | custom-call | flops 2147483648 | bytes 8388608 | tf_op jit(solution)/shard_map/pool/pallas_call | solution.py:153
  85.2 16.6 %all_to_all.15 = bf16[16,64,128]{2,1,0:T(8,128)(2,1)S(1)} all-to-all(bf16[16,64,128]{2,1,0:T(8,128)(2,1)S(1)} %bitcast.17), channel_id=1, replica_groups=mesh['shard'=64,'chip'=8,'core'=2] {'core','chip'}, dimensions={0} | all-to-all | bytes 524288 | tf_op jit(solution)/shard_map/all_to_all | solution.py:229
  101.9 0.0 copy-done
  101.9 0.0 copy-done.1
  101.9 0.9 update.1
  102.8 14.9 %all_to_all.16 = bf16[8,64,256]{2,1,0:T(8,128)(2,1)S(1)} all-to-all(bf16[8,64,256]{2,1,0:T(8,128)(2,1)S(1)} %get-tuple-element.8), channel_id=1, replica_groups=mesh['shard'=64,'chip'=8,'core'=2] {'chip'}, dimensions={0} | all-to-all | bytes 524288 | tf_op jit(solution)/shard_map/all_to_all | solution.py:235
  117.7 3.9 %all-gather = bf16[16,64,256]{2,1,0:T(8,128)(2,1)S(1)} all-gather(bf16[8,64,256]{2,1,0:T(8,128)(2,1)S(1)} %all_to_all.16), channel_id=2, replica_groups=mesh['shard'=64,'chip'=8,'core'=2] {'core'}, dimensions={0}, use_global_device_ids=true | all-gather | bytes 786432 | tf_op jit(solution)/shard_map/all_gather | solution.py:236
  121.6 0.8 copy.9
  (1 shorter events, 0.0 us)
Async XLA Ops:
  3.3 25.4 %copy-start.2 = (s32[1,1,8,4096]{3,2,1,0:T(8,128)S(1)}, s32[1,1,8,4096]{3,2,1,0:T(8,128)}, u32[]{:S(2)}) copy-start(s32[1,1,8,4096]{3,2,1,0:T(8,128)} %param.6) | copy-start | bytes 393220
  3.3 25.4 %copy-start.3 = (s32[1,1,4096]{2,1,0:T(1,128)S(1)}, s32[1,1,4096]{2,1,0:T(1,128)}, u32[]{:S(2)}) copy-start(s32[1,1,4096]{2,1,0:T(1,128)} %param.7) | copy-start | bytes 49156
  3.3 77.5 %all-to-all-start = ((bf16[128,64,128]{2,1,0:T(8,128)(2,1)}), bf16[128,64,128]{2,1,0:T(8,128)(2,1)S(1)}, u32[]{:S(2)}, u32[]{:S(2)}) async-start(bf16[128,64,128]{2,1,0:T(8,128)(2,1)} %bitcast.20), calls=%async_computation | async-start | bytes 4194304 | tf_op jit(solution)/shard_map/all_to_all | solution.py:220
  80.8 21.1 %copy-start = (f32[64,256]{1,0:T(8,128)S(1)}, f32[64,256]{1,0:T(8,128)}, u32[]{:S(2)}) copy-start(f32[64,256]{1,0:T(8,128)} %rows_ref.1) | copy-start | bytes 196612
  80.8 21.1 %copy-start.1 = (f32[64]{0:T(128)S(1)}, f32[64]{0:T(128)}, u32[]{:S(2)}) copy-start(f32[64]{0:T(128)} %param.9) | copy-start | bytes 772

commit v6 on v5

--- a/solution.py
+++ b/solution.py
@@ -9,7 +9,7 @@
 STEP_RATE = 0.5
 EPSILON = 1e-08
 CORES = 2
-COUNT = jnp.float8_e4m3fn
+COUNT = jnp.int4
 VMEM = 56 * 1024 * 1024
 
 
@@ -63,11 +63,11 @@
 def count_kernel(ids_ref, counts_ref):
     positions = ids_ref.shape[1]
     blocks, _, depth, slab = counts_ref.shape
-    tall, lanes = 32, 128
+    tall, lanes = 64, 128
     ids = ids_ref[0].T
     lane = lax.broadcasted_iota(jnp.int32, (tall, lanes), 1).astype(jnp.int16)
-    one = jnp.ones((tall, lanes), jnp.bfloat16)
-    zero = jnp.zeros((tall, lanes), jnp.bfloat16)
+    one = jnp.full((tall, lanes), -1, jnp.int16)
+    zero = jnp.zeros((tall, lanes), jnp.int16)
     for block in range(blocks):
         for low in range(0, depth, tall):
             first = block * depth + low
@@ -138,7 +138,7 @@
         elif i < pieces - 1:
             total_ref[...] += product
         else:
-            pooled = (total_ref[...] + product).T.astype(out_ref.dtype)
+            pooled = (-total_ref[...] - product).T.astype(out_ref.dtype)
             cores, chips, share, _ = out_ref.shape
             for core in range(cores):
                 for chip in range(chips):
@@ -146,7 +146,7 @@
                     out_ref[core, chip] = pooled[first : first + share]
 
 
-def pool(counts, arrived, share, pieces=8):
+def pool(counts, arrived, share, pieces=4):
     samples, width = arrived.shape
     slab = counts.shape[1]
     depth = samples // pieces

time: 124 us -> 124 us (level)
  transfers between devices with their start and end apart: 1 -> 1, of which waited for: 1 -> 1; matrix products, arithmetic and copies ran while one was open for 0% -> 0% of each run, Pallas kernels for 20% -> 19%
where the time goes in v6:
time: 124 us; the launch traced here: 122 us
  blocking collectives  38.1 us (31%)
  Pallas kernels  31.2 us (25%)
  waiting for transfers between devices  25.9 us (21%)
  starting transfers between devices  25.4 us (20%)
    all_to_all x1, waiting for transfers between devices, shards(): lax.all_to_all(outgoing.reshape(features * CORES, mine, half), ('shard',...  25.9 us
    all_to_all x1, starting transfers between devices, shards(): lax.all_to_all(outgoing.reshape(features * CORES, mine, half), ('shard',...  25.4 us
    pallas_call x1, Pallas kernels, count_matrix(): pl.pallas_call(count_kernel, grid=(cores, samples // (blocks * depth)), i...  23.6 us
    all_to_all x1, blocking collectives, shards(): lax.all_to_all(partial.reshape(SLAB // share, share, half), ('core', 'chi...  16.6 us
    all_to_all x1, blocking collectives, shards(): alike = lax.all_to_all(fresh, 'chip', 0, 0, tiled=True)  14.9 us
    pallas_call x1, Pallas kernels, pool(): pl.pallas_call(pool_kernel, in_specs=[pl.BlockSpec(memory_space=pl.ANY)]...  4.15 us
    all_gather x1, blocking collectives, shards(): pairs = lax.all_gather(alike, 'core', axis=0, tiled=False)  3.93 us
    all_gather x1, blocking collectives, shards(): lax.all_gather(ids, 'core', axis=0, tiled=False)  2.66 us
  transfers between devices with their start and end apart: 1, of which 1 were waited for; matrix products, arithmetic and copies ran while one was open for 0% of the time, Pallas kernels for 19%

profile of v6, /device:TPU:1, one launch (start us, length us, event | category | flops | bytes accessed | tf_op | source)
XLA Modules:
  0.0 122.1 jit_solution(221571765876064117)
XLA Ops:
  0.6 2.6 %spread.1 = bf16[64,2,64,128]{3,2,1,0:T(8,128)(2,1)} custom-call(bf16[64,64,256]{2,1,0:T(8,128)(2,1)} %bitcast.21), custom_call_target="tpu_custom_call" | custom-call | tf_op jit(solution)/shard_map/spread/pallas_call | solution.py:47
  3.2 0.0 copy-start.2
  3.2 0.0 copy-start.3
  3.3 25.4 %all-to-all-start = ((bf16[128,64,128]{2,1,0:T(8,128)(2,1)}), bf16[128,64,128]{2,1,0:T(8,128)(2,1)S(1)}, u32[]{:S(2)}, u32[]{:S(2)}) async-start(bf16[128,64,128]{2,1,0:T(8,128)(2,1)} %bitcast.19), calls=%async_computation | async-start | bytes 4194304 | tf_op jit(solution)/shard_map/all_to_all | solution.py:220
  28.6 0.0 copy-done.2
  28.7 0.0 copy-done.3
  28.7 2.7 %all_gather.10.ids_ref = s32[2,8,4096]{2,1,0:T(8,128)} all-gather(s32[1,8,4096]{2,1,0:T(8,128)S(1)} %bitcast_select_fusion), channel_id=1, replica_groups=mesh['shard'=64,'chip'=8,'core'=2] {'core'}, dimensions={0}, use_global_device_ids=true | all-gather | bytes 393216 | tf_op jit(solution)/shard_map/all_gather | solution.py:225
  31.4 23.6 %counts.1 = s4[64,2,64,1024]{3,2,1,0:T(64,128)(8,1)E(4)} custom-call(s32[2,8,4096]{2,1,0:T(8,128)} %all_gather.10.ids_ref), custom_call_target="tpu_custom_call" | custom-call | flops 134217728 | bytes 8388608 | tf_op jit(solution)/shard_map/counts/pallas_call | solution.py:93
  54.9 25.9 %all-to-all-done = bf16[128,64,128]{2,1,0:T(8,128)(2,1)S(1)} async-done(((bf16[128,64,128]{2,1,0:T(8,128)(2,1)}), bf16[128,64,128]{2,1,0:T(8,128)(2,1)S(1)}, u32[]{:S(2)}, u32[]{:S(2)}) %all-to-all-start) | async-done | bytes 2097184 | tf_op jit(solution)/shard_map/all_to_all | solution.py:220
  80.8 0.0 copy-start
  80.8 0.0 copy-start.1
  80.8 4.2 %pool.1 = bf16[2,8,64,128]{3,2,1,0:T(8,128)(2,1)S(1)} custom-call(s4[8192,1024]{1,0:T(64,128)(8,1)E(4)} %bitcast.20, bf16[8192,128]{1,0:T(8,128)(2,1)S(1)} %bitcast.15), custom_call_target="tpu_custom_call" | custom-call | flops 2147483648 | bytes 8388608 | tf_op jit(solution)/shard_map/pool/pallas_call | solution.py:153
  85.0 16.6 %all_to_all.15 = bf16[16,64,128]{2,1,0:T(8,128)(2,1)S(1)} all-to-all(bf16[16,64,128]{2,1,0:T(8,128)(2,1)S(1)} %bitcast.17), channel_id=1, replica_groups=mesh['shard'=64,'chip'=8,'core'=2] {'core','chip'}, dimensions={0} | all-to-all | bytes 524288 | tf_op jit(solution)/shard_map/all_to_all | solution.py:229
  101.6 0.0 copy-done
  101.6 0.0 copy-done.1
  101.6 0.9 update.1
  102.5 14.9 %all_to_all.16 = bf16[8,64,256]{2,1,0:T(8,128)(2,1)S(1)} all-to-all(bf16[8,64,256]{2,1,0:T(8,128)(2,1)S(1)} %get-tuple-element.8), channel_id=1, replica_groups=mesh['shard'=64,'chip'=8,'core'=2] {'chip'}, dimensions={0} | all-to-all | bytes 524288 | tf_op jit(solution)/shard_map/all_to_all | solution.py:235
  117.4 3.9 %all-gather = bf16[16,64,256]{2,1,0:T(8,128)(2,1)S(1)} all-gather(bf16[8,64,256]{2,1,0:T(8,128)(2,1)S(1)} %all_to_all.16), channel_id=2, replica_groups=mesh['shard'=64,'chip'=8,'core'=2] {'core'}, dimensions={0}, use_global_device_ids=true | all-gather | bytes 786432 | tf_op jit(solution)/shard_map/all_gather | solution.py:236
  121.3 0.8 copy.9
  (1 shorter events, 0.0 us)
Async XLA Ops:
  3.2 25.4 %copy-start.2 = (s32[1,1,8,4096]{3,2,1,0:T(8,128)S(1)}, s32[1,1,8,4096]{3,2,1,0:T(8,128)}, u32[]{:S(2)}) copy-start(s32[1,1,8,4096]{3,2,1,0:T(8,128)} %param.6) | copy-start | bytes 393220
  3.2 25.4 %copy-start.3 = (s32[1,1,4096]{2,1,0:T(1,128)S(1)}, s32[1,1,4096]{2,1,0:T(1,128)}, u32[]{:S(2)}) copy-start(s32[1,1,4096]{2,1,0:T(1,128)} %param.7) | copy-start | bytes 49156
  3.3 77.5 %all-to-all-start = ((bf16[128,64,128]{2,1,0:T(8,128)(2,1)}), bf16[128,64,128]{2,1,0:T(8,128)(2,1)S(1)}, u32[]{:S(2)}, u32[]{:S(2)}) async-start(bf16[128,64,128]{2,1,0:T(8,128)(2,1)} %bitcast.19), calls=%async_computation | async-start | bytes 4194304 | tf_op jit(solution)/shard_map/all_to_all | solution.py:220
  80.8 20.8 %copy-start = (f32[64,256]{1,0:T(8,128)S(1)}, f32[64,256]{1,0:T(8,128)}, u32[]{:S(2)}) copy-start(f32[64,256]{1,0:T(8,128)} %rows_ref.1) | copy-start | bytes 196612
  80.8 20.8 %copy-start.1 = (f32[64]{0:T(128)S(1)}, f32[64]{0:T(128)}, u32[]{:S(2)}) copy-start(f32[64]{0:T(128)} %param.9) | copy-start | bytes 772

commit v7 on v6

--- a/solution.py
+++ b/solution.py
@@ -9,6 +9,7 @@
 STEP_RATE = 0.5
 EPSILON = 1e-08
 CORES = 2
+CUTS = (0, 1, 4, 8, 12, 16)
 COUNT = jnp.int4
 VMEM = 56 * 1024 * 1024
 
@@ -107,20 +108,18 @@
 
 
 def pool_kernel(counts_hbm, arrived_hbm, out_ref, counts_ref, arrived_ref, total_ref, sems):
-    pieces = counts_ref.shape[0]
-    depth = counts_ref.shape[1]
-
-    def fetch(i):
-        return (
-            pltpu.make_async_copy(
-                counts_hbm.at[pl.ds(i * depth, depth)], counts_ref.at[i], sems.at[0, i]
-            ),
-            pltpu.make_async_copy(
-                arrived_hbm.at[pl.ds(i * depth, depth)], arrived_ref.at[i], sems.at[1, i]
-            ),
+    samples = counts_ref.shape[0]
+    edges = [samples * cut // 16 for cut in CUTS]
+    pieces = len(CUTS) - 1
+    copies = []
+    for i in range(pieces):
+        mine = pl.ds(edges[i], edges[i + 1] - edges[i])
+        copies.append(
+            (
+                pltpu.make_async_copy(counts_hbm.at[mine], counts_ref.at[mine], sems.at[0, i]),
+                pltpu.make_async_copy(arrived_hbm.at[mine], arrived_ref.at[mine], sems.at[1, i]),
+            )
         )
-
-    copies = [fetch(i) for i in range(pieces)]
     for pair in copies:
         for copy in pair:
             copy.start()
@@ -128,8 +127,8 @@
         for copy in pair:
             copy.wait()
         product = lax.dot_general(
-            arrived_ref[i],
-            counts_ref[i].astype(jnp.bfloat16),
+            arrived_ref[edges[i] : edges[i + 1]],
+            counts_ref[edges[i] : edges[i + 1]].astype(jnp.bfloat16),
             (((0,), (0,)), ((), ())),
             preferred_element_type=jnp.float32,
         )
@@ -146,10 +145,9 @@
                     out_ref[core, chip] = pooled[first : first + share]
 
 
-def pool(counts, arrived, share, pieces=4):
+def pool(counts, arrived, share):
     samples, width = arrived.shape
     slab = counts.shape[1]
-    depth = samples // pieces
     return pl.pallas_call(
         pool_kernel,
         in_specs=[pl.BlockSpec(memory_space=pl.ANY)] * 2,
@@ -158,10 +156,10 @@
             (CORES, slab // share // CORES, share, width), jnp.bfloat16
         ),
         scratch_shapes=[
-            pltpu.VMEM((pieces, depth, slab), counts.dtype),
-            pltpu.VMEM((pieces, depth, width), arrived.dtype),
+            pltpu.VMEM((samples, slab), counts.dtype),
+            pltpu.VMEM((samples, width), arrived.dtype),
             pltpu.VMEM((width, slab), jnp.float32),
-            pltpu.SemaphoreType.DMA((2, pieces)),
+            pltpu.SemaphoreType.DMA((2, len(CUTS) - 1)),
         ],
         compiler_params=pltpu.CompilerParams(vmem_limit_bytes=VMEM - 8 * 1024 * 1024),
         cost_estimate=pl.CostEstimate(

time: 124 us -> 124 us (level)
  no operation moved by 1% of the time
where the time goes in v7:
time: 124 us; the launch traced here: 122 us
  blocking collectives  38.1 us (31%)
  Pallas kernels  31.1 us (25%)
  waiting for transfers between devices  25.9 us (21%)
  starting transfers between devices  25.4 us (20%)
    all_to_all x1, waiting for transfers between devices, shards(): lax.all_to_all(outgoing.reshape(features * CORES, mine, half), ('shard',...  25.9 us
    all_to_all x1, starting transfers between devices, shards(): lax.all_to_all(outgoing.reshape(features * CORES, mine, half), ('shard',...  25.4 us
    pallas_call x1, Pallas kernels, count_matrix(): pl.pallas_call(count_kernel, grid=(cores, samples // (blocks * depth)), i...  23.6 us
    all_to_all x1, blocking collectives, shards(): lax.all_to_all(partial.reshape(SLAB // share, share, half), ('core', 'chi...  16.6 us
    all_to_all x1, blocking collectives, shards(): alike = lax.all_to_all(fresh, 'chip', 0, 0, tiled=True)  14.9 us
    pallas_call x1, Pallas kernels, pool(): pl.pallas_call(pool_kernel, in_specs=[pl.BlockSpec(memory_space=pl.ANY)]...  4.08 us
    all_gather x1, blocking collectives, shards(): pairs = lax.all_gather(alike, 'core', axis=0, tiled=False)  3.93 us
    all_gather x1, blocking collectives, shards(): lax.all_gather(ids, 'core', axis=0, tiled=False)  2.66 us
  transfers between devices with their start and end apart: 1, of which 1 were waited for; matrix products, arithmetic and copies ran while one was open for 0% of the time, Pallas kernels for 19%

profile of v7, /device:TPU:1, one launch (start us, length us, event | category | flops | bytes accessed | tf_op | source)
XLA Modules:
  0.0 122.0 jit_solution(13012662537196669218)
XLA Ops:
  0.6 2.6 %spread.1 = bf16[64,2,64,128]{3,2,1,0:T(8,128)(2,1)} custom-call(bf16[64,64,256]{2,1,0:T(8,128)(2,1)} %bitcast.21), custom_call_target="tpu_custom_call" | custom-call | tf_op jit(solution)/shard_map/spread/pallas_call | solution.py:48
  3.2 0.0 copy-start.2
  3.2 0.0 copy-start.3
  3.3 25.4 %all-to-all-start = ((bf16[128,64,128]{2,1,0:T(8,128)(2,1)}), bf16[128,64,128]{2,1,0:T(8,128)(2,1)S(1)}, u32[]{:S(2)}, u32[]{:S(2)}) async-start(bf16[128,64,128]{2,1,0:T(8,128)(2,1)} %bitcast.19), calls=%async_computation | async-start | bytes 4194304 | tf_op jit(solution)/shard_map/all_to_all | solution.py:218
  28.6 0.0 copy-done.2
  28.7 0.0 copy-done.3
  28.7 2.7 %all_gather.10.ids_ref = s32[2,8,4096]{2,1,0:T(8,128)} all-gather(s32[1,8,4096]{2,1,0:T(8,128)S(1)} %bitcast_select_fusion), channel_id=1, replica_groups=mesh['shard'=64,'chip'=8,'core'=2] {'core'}, dimensions={0}, use_global_device_ids=true | all-gather | bytes 393216 | tf_op jit(solution)/shard_map/all_gather | solution.py:223
  31.4 23.6 %counts.1 = s4[64,2,64,1024]{3,2,1,0:T(64,128)(8,1)E(4)} custom-call(s32[2,8,4096]{2,1,0:T(8,128)} %all_gather.10.ids_ref), custom_call_target="tpu_custom_call" | custom-call | flops 134217728 | bytes 8388608 | tf_op jit(solution)/shard_map/counts/pallas_call | solution.py:94
  54.9 25.9 %all-to-all-done = bf16[128,64,128]{2,1,0:T(8,128)(2,1)S(1)} async-done(((bf16[128,64,128]{2,1,0:T(8,128)(2,1)}), bf16[128,64,128]{2,1,0:T(8,128)(2,1)S(1)}, u32[]{:S(2)}, u32[]{:S(2)}) %all-to-all-start) | async-done | bytes 2097184 | tf_op jit(solution)/shard_map/all_to_all | solution.py:218
  80.8 0.0 copy-start
  80.8 0.0 copy-start.1
  80.8 4.1 %pool.1 = bf16[2,8,64,128]{3,2,1,0:T(8,128)(2,1)S(1)} custom-call(s4[8192,1024]{1,0:T(64,128)(8,1)E(4)} %bitcast.20, bf16[8192,128]{1,0:T(8,128)(2,1)S(1)} %bitcast.15), custom_call_target="tpu_custom_call" | custom-call | flops 2147483648 | bytes 8388608 | tf_op jit(solution)/shard_map/pool/pallas_call | solution.py:151
  84.9 16.6 %all_to_all.15 = bf16[16,64,128]{2,1,0:T(8,128)(2,1)S(1)} all-to-all(bf16[16,64,128]{2,1,0:T(8,128)(2,1)S(1)} %bitcast.17), channel_id=1, replica_groups=mesh['shard'=64,'chip'=8,'core'=2] {'core','chip'}, dimensions={0} | all-to-all | bytes 524288 | tf_op jit(solution)/shard_map/all_to_all | solution.py:227
  101.5 0.0 copy-done
  101.5 0.0 copy-done.1
  101.5 0.9 update.1
  102.4 14.9 %all_to_all.16 = bf16[8,64,256]{2,1,0:T(8,128)(2,1)S(1)} all-to-all(bf16[8,64,256]{2,1,0:T(8,128)(2,1)S(1)} %get-tuple-element.8), channel_id=1, replica_groups=mesh['shard'=64,'chip'=8,'core'=2] {'chip'}, dimensions={0} | all-to-all | bytes 524288 | tf_op jit(solution)/shard_map/all_to_all | solution.py:233
  117.3 3.9 %all-gather = bf16[16,64,256]{2,1,0:T(8,128)(2,1)S(1)} all-gather(bf16[8,64,256]{2,1,0:T(8,128)(2,1)S(1)} %all_to_all.16), channel_id=2, replica_groups=mesh['shard'=64,'chip'=8,'core'=2] {'core'}, dimensions={0}, use_global_device_ids=true | all-gather | bytes 786432 | tf_op jit(solution)/shard_map/all_gather | solution.py:234
  121.2 0.8 copy.9
  (1 shorter events, 0.0 us)
Async XLA Ops:
  3.2 25.4 %copy-start.2 = (s32[1,1,8,4096]{3,2,1,0:T(8,128)S(1)}, s32[1,1,8,4096]{3,2,1,0:T(8,128)}, u32[]{:S(2)}) copy-start(s32[1,1,8,4096]{3,2,1,0:T(8,128)} %param.6) | copy-start | bytes 393220
  3.2 25.4 %copy-start.3 = (s32[1,1,4096]{2,1,0:T(1,128)S(1)}, s32[1,1,4096]{2,1,0:T(1,128)}, u32[]{:S(2)}) copy-start(s32[1,1,4096]{2,1,0:T(1,128)} %param.7) | copy-start | bytes 49156
  3.3 77.5 %all-to-all-start = ((bf16[128,64,128]{2,1,0:T(8,128)(2,1)}), bf16[128,64,128]{2,1,0:T(8,128)(2,1)S(1)}, u32[]{:S(2)}, u32[]{:S(2)}) async-start(bf16[128,64,128]{2,1,0:T(8,128)(2,1)} %bitcast.19), calls=%async_computation | async-start | bytes 4194304 | tf_op jit(solution)/shard_map/all_to_all | solution.py:218
  80.8 20.7 %copy-start = (f32[64,256]{1,0:T(8,128)S(1)}, f32[64,256]{1,0:T(8,128)}, u32[]{:S(2)}) copy-start(f32[64,256]{1,0:T(8,128)} %rows_ref.1) | copy-start | bytes 196612
  80.8 20.7 %copy-start.1 = (f32[64]{0:T(128)S(1)}, f32[64]{0:T(128)}, u32[]{:S(2)}) copy-start(f32[64]{0:T(128)} %param.9) | copy-start | bytes 772
